TPU v7x, 32 devices: a whole 2x2x4 slice. The times are simulated.
32 devices in a mesh: seq: 8 (over z, y), tp: 4 (over x, core).
Axes of the slice: x: 2, y: 2, z: 4, core: 2. Of those that a mesh axis runs over, the one named last changes fastest.
Arguments:
- db_tokens: int32 [4096, 128], P('seq'), may hold values from 0 to 16383
- db_parent: int32 [4096, 128], P('seq'), may hold values from 0 to 126, as said below
- db_depth: int32 [4096, 128], P('seq'), may hold values from 0 to 31, as said below
- nb_rows: int32 [64, 2], P('seq'), may hold values from 0 to 4095, as said below
- seq_start: int32 [64], P('seq'), may hold values 0 or 1
- table: bfloat16 [16384, 1024], P(None, 'tp'), may hold values from -40 to 40
- depth_table: bfloat16 [32, 1024], P(None, 'tp'), may hold values from -3 to 3
- enc_gain: float32 [1024], replicated, may hold values from 0.25 to 1.75
- enc_qkv: bfloat16 [1024, 3, 1024], P('seq', None, 'tp'), may hold values from -0.1875 to 0.1875
- tree_bias: float32 [8], replicated, may hold values from 1 to 4
- enc_wo: bfloat16 [1024, 1024], P('tp', 'seq'), may hold values from -0.1875 to 0.1875
- cond_kv: bfloat16 [4096, 2, 1024], P('seq', None, 'tp'), may hold values from -150 to 150
- queries: bfloat16 [4096, 4096], P('seq', 'tp'), may hold values from -150 to 150
- cca_kv: bfloat16 [1024, 2, 512], P('seq', None, 'tp'), may hold values from -0.1875 to 0.1875
Outputs:
- attended: bfloat16 [4096, 4096], P('seq', 'tp')
Inputs may be any that keep to these rules, and one draw needn't show every extreme that they name: `db_parent`: position 0 of every stored neighbour is its own parent; every other position's parent is one of the three positions just before it. `db_depth`: position 0 has depth 0; every other position has its parent's depth plus one, capped at 31. `nb_rows`: rows 512 * i to 512 * (i + 1) - 1 of the database lie on index i of seq. Of the 16 neighbours of one index's blocks at most 4 lie on any one index; at most 32 neighbours of all blocks lie on one index, and in every draw some index holds exactly 32.
All inputs are finite; a program needn't handle non-finite values. No bound on the sum of `seq_start` on one device may be relied on, other than what follows from the above.
Results may differ from a plain program's by a relative error of at most 0.0223.
The roundings to bfloat16 on the way count: a program that leaves them out, or rounds other values in their place, can miss the bound.
Values may be sent and summed in bfloat16 or wider, within the bound.
A program may use at most 128 MiB of HBM per device.

v0:
```python
import math

import jax
import jax.numpy as jnp
from jax import lax
from jax.sharding import PartitionSpec as P

HD = 128


def from_behind(value, axis, steps):
    count = lax.axis_size(axis)
    initial, last = (max(0, -steps), min(count, count - steps))
    return lax.ppermute(value, axis, [(source, source + steps) for source in range(initial, last)])


def normalize(embedded, gain):
    embedded_f = embedded.astype(jnp.float32)
    return (
        embedded_f
        * lax.rsqrt(jnp.mean(embedded_f * embedded_f, axis=-1, keepdims=True) + 1e-05)
        * gain
    ).astype(jnp.bfloat16)


def encoder_mix(normed, parents, conditioning, w_qkv, bias, head_count):
    unit_count = normed.shape[0]
    length = normed.shape[1]
    blocks = conditioning.shape[0]
    pair_count = unit_count // blocks
    cond_len = conditioning.shape[1]
    score_scale = 1.0 / math.sqrt(HD)
    projected = jnp.einsum(
        "une,eaf->unaf", normed, w_qkv, preferred_element_type=jnp.float32
    ).astype(jnp.bfloat16)
    shaped = projected.reshape(blocks, pair_count, length, 3, head_count, HD)
    query_part = shaped[:, :, :, 0]
    key_part = shaped[:, :, :, 1]
    value_part = shaped[:, :, :, 2]
    cond_keys = conditioning[:, :, 0].reshape(blocks, cond_len, head_count, HD)
    cond_values = conditioning[:, :, 1].reshape(blocks, cond_len, head_count, HD)
    self_scores = (
        jnp.einsum("cpihd,cpjhd->cphij", query_part, key_part, preferred_element_type=jnp.float32)
        * score_scale
    )
    parent_hit = (
        parents.reshape(blocks, pair_count, length)[:, :, :, None]
        == jnp.arange(length, dtype=jnp.float32)[None, None, None, :]
    ).astype(jnp.float32)
    self_scores = self_scores + bias[None, None, :, None, None] * parent_hit[:, :, None]
    cond_scores = (
        jnp.einsum("cpihd,crhd->cphir", query_part, cond_keys, preferred_element_type=jnp.float32)
        * score_scale
    )
    weights = jax.nn.softmax(jnp.concatenate([self_scores, cond_scores], axis=-1), axis=-1).astype(
        jnp.bfloat16
    )
    mixed = jnp.einsum(
        "cphij,cpjhd->cpihd", weights[..., :length], value_part, preferred_element_type=jnp.float32
    )
    mixed = mixed + jnp.einsum(
        "cphir,crhd->cpihd", weights[..., length:], cond_values, preferred_element_type=jnp.float32
    )
    return mixed.astype(jnp.bfloat16).reshape(unit_count, length, head_count * HD)


def attend(query, key_value):
    blocks, key_rows = (key_value.shape[0], key_value.shape[1])
    token_count = query.shape[1]
    head_count = query.shape[2]
    kv_heads = key_value.shape[3] // HD
    group = head_count // kv_heads
    grouped = query.reshape(blocks, token_count, kv_heads, group, HD)
    key_part = key_value[:, :, 0].reshape(blocks, key_rows, kv_heads, HD)
    value_part = key_value[:, :, 1].reshape(blocks, key_rows, kv_heads, HD)
    scores = jnp.einsum(
        "ctkgd,cpkd->ckgtp", grouped, key_part, preferred_element_type=jnp.float32
    ) * (1.0 / math.sqrt(HD))
    weights = jax.nn.softmax(scores, axis=-1).astype(jnp.bfloat16)
    output = jnp.einsum(
        "ckgtp,cpkd->ctkgd", weights, value_part, preferred_element_type=jnp.float32
    ).astype(jnp.bfloat16)
    return output.reshape(blocks, token_count, head_count, HD)


def shards(
    db_tokens,
    db_parent,
    db_depth,
    nb_rows,
    seq_start,
    table,
    depth_table,
    enc_gain,
    enc_qkv,
    tree_bias,
    enc_wo,
    cond_kv,
    queries,
    cca_kv,
):
    seq_size = lax.axis_size("seq")
    tp_size = lax.axis_size("tp")
    block_count, pair_count = nb_rows.shape
    unit_count = block_count * pair_count
    stored = db_tokens.shape[0]
    length = db_tokens.shape[1]
    slot_count = max(1, 2 * unit_count // seq_size)
    flat_rows = nb_rows.reshape(unit_count)
    holder = flat_rows // stored
    local_row = flat_rows % stored
    ordering = jnp.arange(unit_count, dtype=jnp.int32)
    earlier = jnp.sum(
        ((holder[:, None] == holder[None, :]) & (ordering[:, None] > ordering[None, :])).astype(
            jnp.int32
        ),
        axis=1,
    )
    target = holder * slot_count + earlier
    places = jnp.arange(seq_size * slot_count, dtype=jnp.int32)
    request = jnp.sum(
        jnp.where(target[None, :] == places[:, None], local_row[None, :], 0), axis=1
    ).reshape(seq_size, slot_count)
    wanted = lax.all_to_all(request, "seq", split_axis=0, concat_axis=0, tiled=True)
    tokens = jnp.take(db_tokens, wanted, axis=0)
    depths = jnp.take(db_depth, wanted, axis=0)
    parents = jnp.take(db_parent, wanted, axis=0).astype(jnp.bfloat16)
    embedded = (
        jnp.take(table, tokens, axis=0).astype(jnp.float32)
        + jnp.take(depth_table, depths, axis=0).astype(jnp.float32)
    ).astype(jnp.bfloat16)
    fetched = lax.all_to_all(embedded, "seq", split_axis=0, concat_axis=0, tiled=True)
    fetched_parents = lax.all_to_all(parents, "seq", split_axis=0, concat_axis=0, tiled=True)
    embedded = jnp.take(
        fetched.reshape((seq_size * slot_count,) + fetched.shape[2:]), target, axis=0
    )
    parents = jnp.take(
        fetched_parents.reshape(seq_size * slot_count, length), target, axis=0
    ).astype(jnp.float32)
    row_qkv, row_out = (
        lax.all_gather(enc_qkv, "seq", axis=0, tiled=True),
        lax.all_gather(enc_wo, "seq", axis=1, tiled=True),
    )
    cond_columns = cond_kv.shape[2]
    cond_len = cond_kv.shape[0] // block_count
    full_width = row_qkv.shape[0]
    unit_share = unit_count // tp_size
    cond_flat = cond_kv.reshape(block_count, cond_len * 2, cond_columns)
    own_units, own_cond = (
        lax.all_to_all(embedded, "tp", split_axis=0, concat_axis=2, tiled=True),
        lax.all_to_all(cond_flat, "tp", split_axis=0, concat_axis=2, tiled=True),
    )
    full_qkv, full_out = (
        lax.all_gather(row_qkv, "tp", axis=2, tiled=True),
        lax.all_gather(row_out, "tp", axis=0, tiled=True),
    )
    own_parents = lax.dynamic_slice_in_dim(
        parents, lax.axis_index("tp") * unit_share, unit_share, 0
    )
    conditioning = own_cond.reshape(own_cond.shape[0], cond_len, 2, full_width)
    normed = normalize(own_units, enc_gain)
    mixed = encoder_mix(
        normed, own_parents, conditioning, full_qkv, tree_bias, tree_bias.shape[0]
    ).reshape(unit_share * length, full_width)
    increment = jnp.dot(mixed, full_out, preferred_element_type=jnp.float32)
    encoded_part = (
        own_units.reshape(unit_share * length, full_width).astype(jnp.float32) + increment
    ).astype(jnp.bfloat16)
    encoded = lax.all_gather(encoded_part, "tp", axis=0, tiled=True)
    kv_weight = lax.all_gather(cca_kv, "seq", axis=0, tiled=True)
    key_rows = pair_count * length
    keys_values = jnp.einsum(
        "re,eaf->raf", encoded, kv_weight, preferred_element_type=jnp.float32
    ).astype(jnp.bfloat16)
    keys_values = keys_values.reshape(block_count, key_rows, 2, keys_values.shape[2])
    carried = from_behind(keys_values[block_count - 1], "seq", 1)
    previous = jnp.concatenate([carried[None], keys_values[: block_count - 1]], axis=0)
    head_queries = queries.shape[1] // HD
    query_heads = queries.reshape(block_count, cond_len, head_queries, HD)
    leading = attend(query_heads[:, : cond_len - 1], previous)
    trailing = attend(query_heads[:, cond_len - 1 :], keys_values)
    block_index = lax.axis_index("seq") * block_count + jnp.arange(block_count, dtype=jnp.int32)
    allowed = (block_index > 0) & (seq_start == 0)
    leading = jnp.where(allowed[:, None, None, None], leading, jnp.zeros_like(leading))
    attended = jnp.concatenate([leading, trailing], axis=1)
    return attended.reshape(block_count * cond_len, head_queries * HD)


def solution(mesh):
    in_specs = (
        P("seq", None),
        P("seq", None),
        P("seq", None),
        P("seq", None),
        P("seq"),
        P(None, "tp"),
        P(None, "tp"),
        P(),
        P("seq", None, "tp"),
        P(),
        P("tp", "seq"),
        P("seq", None, "tp"),
        P("seq", "tp"),
        P("seq", None, "tp"),
    )
    out_specs = P("seq", "tp")
    return jax.shard_map(shards, mesh=mesh, in_specs=in_specs, out_specs=out_specs, check_vma=False)
```

profile of v0, /device:TPU:13, one launch (start us, length us, event | category | flops | bytes accessed | tf_op | source)
XLA Modules:
  0.0 308.6 jit_solution(14261789735247770412)
XLA Ops:
  6.5 0.7 all-gather.5.cloned.1.call-update
  7.3 46.4 %all-gather.5.cloned.1.call-done = bf16[1024,3,256]{2,0,1:T(8,128)(2,1)} async-done(((bf16[128,3,256]{2,0,1:T(8,128)(2,1)}), bf16[1024,3,256]{2,0,1:T(8,128)(2,1)}) %all-gather.5.cloned.1.call-update) | async-done | bytes 1572880 | tf_op jit(solution)/shard_map/all_gather | solution.py:141
  53.7 0.8 copy.117
  54.6 0.2 convert_reduce_fusion
  54.9 7.6 %all_to_all.46 = s32[8,1,4]{2,1,0:T(1,128)S(1)} all-to-all(s32[8,1,4]{2,1,0:T(1,128)S(1)} %bitcast.227), channel_id=1, replica_groups=mesh['seq'=8,'tp'=4] {'seq'}, dimensions={0} | all-to-all | bytes 256 | tf_op jit(solution)/shard_map/all_to_all | solution.py:124
  62.8 0.6 gather_fusion.4
  63.4 1.6 gather_fusion.5
  65.1 0.6 gather_fusion.6
  65.7 0.7 select_convert_fusion
  66.3 5.3 %all-to-all-start.3 = ((bf16[8,4,128]{2,1,0:T(4,128)(2,1)}), bf16[8,4,128]{2,1,0:T(4,128)(2,1)S(1)}, u32[]{:S(2)}, u32[]{:S(2)}) async-start(bf16[8,4,128]{2,1,0:T(4,128)(2,1)} %select_convert_fusion), calls=%async_computation.3 | async-start | bytes 16384 | tf_op jit(solution)/shard_map/all_to_all | solution.py:133
  71.8 17.5 %gather_fusion = bf16[4096,256]{1,0:T(8,128)(2,1)S(1)} fusion(bf16[16384,256]{1,0:T(8,128)(2,1)} %param.21, s32[4096]{0:T(1024)S(1)} %broadcast_clamp_fusion.1), kind=kCustom, calls=%fused_computation.3 | custom fusion | bytes 4210688 | tf_op jit(solution)/shard_map/jit(_take)/gather | solution.py:129
  89.3 0.7 copy-done.2
  90.0 17.0 %gather_fusion.1 = bf16[4096,256]{1,0:T(8,128)(2,1)} fusion(bf16[32,256]{1,0:T(8,128)(2,1)S(1)} %copy-done.2, s32[4096]{0:T(1024)S(1)} %broadcast_clamp_fusion), kind=kCustom, calls=%fused_computation.4 | custom fusion | bytes 4210688 | tf_op jit(solution)/shard_map/jit(_take)/gather | solution.py:130
  107.0 4.4 %add_convert_fusion = bf16[8,4,128,256]{3,2,1,0:T(8,128)(2,1)} fusion(bf16[8,4,128,256]{3,2,1,0:T(8,128)(2,1)} %bitcast.201, bf16[8,4,128,256]{3,2,1,0:T(8,128)(2,1)S(1)} %bitcast.200, pred[8,4,128]{2,1,0:T(4,128)(4,1)S(1)} %get-tuple-element.17, pred[8,4,128]{2,1,0:T(4,128)(4,1)S(1)} %get-tuple-element.10), kind=kLoop, calls=%fused_computation.15 | loop fusion | flops 6291456 | bytes 6299648 | tf_op jit(solution)/shard_map/convert_element_type | solution.py:131
  111.5 5.6 %all-to-all-start.1 = ((bf16[8,4,128,256]{3,2,1,0:T(8,128)(2,1)}), bf16[8,4,128,256]{3,2,1,0:T(8,128)(2,1)S(1)}, u32[]{:S(2)}, u32[]{:S(2)}) async-start(bf16[8,4,128,256]{3,2,1,0:T(8,128)(2,1)} %add_convert_fusion), calls=%async_computation.1 | async-start | bytes 4194304 | tf_op jit(solution)/shard_map/all_to_all | solution.py:132
  117.1 61.1 %all_gather.20 = bf16[256,1024]{1,0:T(8,128)(2,1)} all-gather(bf16[256,128]{1,0:T(8,128)(2,1)S(1)} %copy-done.9), channel_id=1, replica_groups=mesh['seq'=8,'tp'=4] {'seq'}, dimensions={1}, use_global_device_ids=true | all-gather | bytes 589824 | tf_op jit(solution)/shard_map/all_gather | solution.py:142
  178.3 1.0 reshape.321
  179.4 0.6 gather_fusion.3
  180.0 6.0 %all-to-all-start.4 = ((bf16[8,128,256]{2,1,0:T(8,128)(2,1)}), bf16[8,128,256]{2,1,0:T(8,128)(2,1)}, u32[]{:S(2)}, u32[]{:S(2)}) async-start(bf16[8,128,256]{2,1,0:T(8,128)(2,1)} %reshape.321), calls=%async_computation.4 | async-start | bytes 1048576 | tf_op jit(solution)/shard_map/all_to_all | solution.py:151
  186.1 0.6 gather_fusion.2
  186.7 1.1 broadcast_select_fusion
  187.9 6.3 %all-to-all-done.4 = bf16[8,128,256]{2,1,0:T(8,128)(2,1)} async-done(((bf16[8,128,256]{2,1,0:T(8,128)(2,1)}), bf16[8,128,256]{2,1,0:T(8,128)(2,1)}, u32[]{:S(2)}, u32[]{:S(2)}) %all-to-all-start.4) | async-done | bytes 524320 | tf_op jit(solution)/shard_map/all_to_all | solution.py:151
  194.1 4.4 %all-to-all-start.2 = ((bf16[16,128,256]{2,1,0:T(8,128)(2,1)}), bf16[16,128,256]{2,1,0:T(8,128)(2,1)S(1)}, u32[]{:S(2)}, u32[]{:S(2)}) async-start(bf16[16,128,256]{2,1,0:T(8,128)(2,1)} %broadcast_select_fusion), calls=%async_computation.2 | async-start | bytes 2097152 | tf_op jit(solution)/shard_map/all_to_all | solution.py:150
  198.5 0.7 fusion.49
  199.2 1.4 copy.133
  200.7 0.2 reshape.322
  200.9 2.2 slice_reduce_fusion
  203.2 0.7 bitcast_bitcast_fusion
  203.9 14.1 %all-to-all-done.2 = bf16[16,128,256]{2,1,0:T(8,128)(2,1)S(1)} async-done(((bf16[16,128,256]{2,1,0:T(8,128)(2,1)}), bf16[16,128,256]{2,1,0:T(8,128)(2,1)S(1)}, u32[]{:S(2)}, u32[]{:S(2)}) %all-to-all-start.2) | async-done | bytes 1048608 | tf_op jit(solution)/shard_map/all_to_all | solution.py:150
  218.0 0.2 convert_element_type.124
  218.3 2.0 copy.126
  220.3 0.3 multiply_reduce_fusion
  220.7 1.9 fusion.18
  222.6 1.4 copy.125
  223.9 1.8 copy.165
  225.8 6.5 %fusion.10 = bf16[4,128,3,1024]{3,1,2,0:T(8,128)(2,1)S(1)} fusion(bf16[1024,3,1024]{2,0,1:T(8,128)(2,1)} %all-gather.7.cloned.1.call-done, bf16[4,128,1024]{1,2,0:T(8,128)(2,1)S(1)} %fusion.18), kind=kOutput, calls=%fused_computation.21 | convolution fusion | flops 3222798336 | bytes 10485760 | tf_op jit(solution)/shard_map/une,eaf->unaf/dot_general | solution.py:33
  232.2 0.8 copy.166
  233.1 1.2 fusion.59
  234.2 0.8 copy.161
  235.1 0.5 fusion.61
  235.6 0.7 copy-done.5
  236.3 0.9 fusion.60
  237.2 0.5 fusion.13
  237.7 0.6 divide_convert_fusion.1
  238.3 0.4 fusion.34
  238.8 0.5 copy-done.6
  239.3 0.5 fusion.16
  239.8 1.5 copy.140
  241.2 4.2 %add_convert_fusion.1 = bf16[512,1024]{1,0:T(8,128)(2,1)} fusion(f32[512,1024]{1,0:T(8,128)S(1)} %bitcast.209, bf16[1024,1024]{1,0:T(8,128)(2,1)} %all-gather.9.cloned.1.call-done, bf16[64,8,8,128]{3,2,1,0:T(8,128)(2,1)} %bitcast.213), kind=kOutput, calls=%fused_computation.31 | convolution fusion | flops 1074790400 | bytes 6291456 | tf_op jit(solution)/shard_map/dot_general | solution.py:165
  245.5 0.3 copy.170
  245.9 0.3 copy-done.14
  246.2 28.1 %all_gather.23 = bf16[1024,2,128]{2,0,1:T(8,128)(2,1)S(1)} all-gather(bf16[128,2,128]{2,0,1:T(8,128)(2,1)S(1)} %copy.141), channel_id=1, replica_groups=mesh['seq'=8,'tp'=4] {'seq'}, dimensions={0}, use_global_device_ids=true | all-gather | bytes 589824 | tf_op jit(solution)/shard_map/all_gather | solution.py:170
  274.3 11.2 %all-gather.11.cloned.1.call-done = bf16[2048,1024]{1,0:T(8,128)(2,1)} async-done(((bf16[512,1024]{1,0:T(8,128)(2,1)}), bf16[2048,1024]{1,0:T(8,128)(2,1)}) %all-gather.11.cloned.1.call-update) | async-done | bytes 4194320 | tf_op jit(solution)/shard_map/all_gather | solution.py:169
  285.5 3.4 %fusion.7 = bf16[2048,2,128]{2,0,1:T(8,128)(2,1)S(1)} fusion(bf16[1024,2,128]{2,0,1:T(8,128)(2,1)S(1)} %all_gather.23, bf16[2048,1024]{1,0:T(8,128)(2,1)} %all-gather.11.cloned.1.call-done), kind=kOutput, calls=%fused_computation.20 | convolution fusion | flops 1074266112 | bytes 5767168 | tf_op jit(solution)/shard_map/re,eaf->raf/dot_general | solution.py:172
  289.1 3.1 %collective-permute-start = (bf16[256,2,128]{2,0,1:T(8,128)(2,1)S(1)}, bf16[256,2,128]{2,0,1:T(8,128)(2,1)S(1)}, u32[]{:S(2)}, u32[]{:S(2)}) collective-permute-start(bf16[256,2,128]{2,0,1:T(8,128)(2,1)S(1)} %slice.86), channel_id=1, source_target_pairs={{0,4},{4,8},{8,12},{12,16},{16,20},{20,24},{24,28},{1,5},{5,9},{9,... | collective-permute-start | bytes 393224 | tf_op jit(solution)/shard_map/ppermute | solution.py:14
  292.2 0.3 fusion.62
  292.5 0.2 fusion.50
  292.7 0.2 fusion.28
  293.0 2.8 collective-permute-done
  295.8 0.8 bitcast_reduce_fusion
  296.6 1.4 fusion.5
  298.0 1.9 fusion.29
  300.1 0.7 copy.145
  300.8 1.2 copy.198
  (70 shorter events, 1.7 us)
Async XLA Ops:
  6.5 56.3 %copy-start = (s32[512,128]{1,0:T(8,128)S(1)}, s32[512,128]{1,0:T(8,128)}, u32[]{:S(2)}) copy-start(s32[512,128]{1,0:T(8,128)} %param.16) | copy-start | bytes 786436
  6.5 58.5 %copy-start.10 = (s32[512,128]{1,0:T(8,128)S(1)}, s32[512,128]{1,0:T(8,128)}, u32[]{:S(2)}) copy-start(s32[512,128]{1,0:T(8,128)} %param.17) | copy-start | bytes 786436
  6.5 47.2 %all-gather.5.cloned.1.call-start = ((), (), s32[]{:S(2)}) async-start(), calls=%async_computation.5 | async-start | bytes 1769472 | tf_op jit(solution)/shard_map/all_gather | solution.py:141
  7.3 218.5 %all-gather.7.cloned.1.call-start = ((), (), s32[]{:S(2)}) async-start(), calls=%async_computation.6 | async-start | bytes 7864320 | tf_op jit(solution)/shard_map/all_gather | solution.py:154
  66.3 45.1 %all-to-all-start.3 = ((bf16[8,4,128]{2,1,0:T(4,128)(2,1)}), bf16[8,4,128]{2,1,0:T(4,128)(2,1)S(1)}, u32[]{:S(2)}, u32[]{:S(2)}) async-start(bf16[8,4,128]{2,1,0:T(4,128)(2,1)} %select_convert_fusion), calls=%async_computation.3 | async-start | bytes 16384 | tf_op jit(solution)/shard_map/all_to_all | solution.py:133
  89.3 0.7 copy-start.2
  111.4 5.6 %copy-start.9 = (bf16[256,128]{1,0:T(8,128)(2,1)S(1)}, bf16[256,128]{1,0:T(8,128)(2,1)}, u32[]{:S(2)}) copy-start(bf16[256,128]{1,0:T(8,128)(2,1)} %param.26) | copy-start | bytes 196612
  111.5 66.9 %copy-start.7 = (bf16[512,2,256]{2,1,0:T(2,128)(2,1)S(1)}, bf16[512,2,256]{2,1,0:T(2,128)(2,1)}, u32[]{:S(2)}) copy-start(bf16[512,2,256]{2,1,0:T(2,128)(2,1)} %param.27) | copy-start | bytes 1572868
  111.5 68.6 %all-to-all-start.1 = ((bf16[8,4,128,256]{3,2,1,0:T(8,128)(2,1)}), bf16[8,4,128,256]{3,2,1,0:T(8,128)(2,1)S(1)}, u32[]{:S(2)}, u32[]{:S(2)}) async-start(bf16[8,4,128,256]{3,2,1,0:T(8,128)(2,1)} %add_convert_fusion), calls=%async_computation.1 | async-start | bytes 4194304 | tf_op jit(solution)/shard_map/all_to_all | solution.py:132
  117.1 124.2 %all-gather.9.cloned.1.call-start = ((), (), s32[]{:S(2)}) async-start(), calls=%async_computation.7 | async-start | bytes 2621440 | tf_op jit(solution)/shard_map/all_gather | solution.py:155
  180.0 14.1 %all-to-all-start.4 = ((bf16[8,128,256]{2,1,0:T(8,128)(2,1)}), bf16[8,128,256]{2,1,0:T(8,128)(2,1)}, u32[]{:S(2)}, u32[]{:S(2)}) async-start(bf16[8,128,256]{2,1,0:T(8,128)(2,1)} %reshape.321), calls=%async_computation.4 | async-start | bytes 1048576 | tf_op jit(solution)/shard_map/all_to_all | solution.py:151
  194.1 23.9 %all-to-all-start.2 = ((bf16[16,128,256]{2,1,0:T(8,128)(2,1)}), bf16[16,128,256]{2,1,0:T(8,128)(2,1)S(1)}, u32[]{:S(2)}, u32[]{:S(2)}) async-start(bf16[16,128,256]{2,1,0:T(8,128)(2,1)} %broadcast_select_fusion), calls=%async_computation.2 | async-start | bytes 2097152 | tf_op jit(solution)/shard_map/all_to_all | solution.py:150
  198.5 87.0 %all-gather.11.cloned.1.call-start = ((), (), s32[]{:S(2)}) async-start(), calls=%async_computation.8 | async-start | bytes 5242880 | tf_op jit(solution)/shard_map/all_gather | solution.py:169
  218.3 2.4 copy-start.12
  234.2 1.3 copy-start.13
  235.0 1.2 copy-start.5
  235.0 1.3 copy-start.8
  238.3 1.0 copy-start.6
  239.3 2.0 copy-start.3
  241.2 4.3 %copy-start.11 = (bf16[128,2,128]{2,1,0:T(2,128)(2,1)S(1)}, bf16[128,2,128]{2,1,0:T(2,128)(2,1)}, u32[]{:S(2)}) copy-start(bf16[128,2,128]{2,1,0:T(2,128)(2,1)} %param.29) | copy-start | bytes 196612
  241.2 4.3 %copy-start.4 = (bf16[512,1024]{1,0:T(8,128)(2,1)S(1)}, bf16[512,1024]{1,0:T(8,128)(2,1)}, u32[]{:S(2)}) copy-start(bf16[512,1024]{1,0:T(8,128)(2,1)} %param.28) | copy-start | bytes 3145732
  245.5 0.7 copy-start.14
  289.1 6.7 %collective-permute-start = (bf16[256,2,128]{2,0,1:T(8,128)(2,1)S(1)}, bf16[256,2,128]{2,0,1:T(8,128)(2,1)S(1)}, u32[]{:S(2)}, u32[]{:S(2)}) collective-permute-start(bf16[256,2,128]{2,0,1:T(8,128)(2,1)S(1)} %slice.86), channel_id=1, source_target_pairs={{0,4},{4,8},{8,12},{12,16},{16,20},{20,24},{24,28},{1,5},{5,9},{9,... | collective-permute-start | bytes 393224 | tf_op jit(solution)/shard_map/ppermute | solution.py:14
  299.9 2.1 copy-start.1
Sparse Core Ops, SparseCore 0:
  9.5 44.1 all-gather.4
  55.2 47.6 all-gather.6
  178.4 35.9 all-gather.8
  245.6 39.8 all-gather.10
where the time goes:
time: 311 us; the launch traced here: 309 us
  blocking collectives  96.9 us (31%)
  waiting for transfers between devices  81.6 us (26%)
  local copies, waits for them, and re-layouts  59.7 us (19%)
  starting transfers between devices  24.5 us (8%)
  matrix products  19.6 us (6%)
  between operations  13.6 us (4%)
  other arithmetic  12.8 us (4%)
    all_gather x1, blocking collectives, shards(): lax.all_gather(enc_wo, 'seq', axis=1, tiled=True)  61.1 us
    all_gather x1, waiting for transfers between devices, shards(): lax.all_gather(enc_qkv, 'seq', axis=0, tiled=True)  46.4 us
    all_gather x1, blocking collectives, shards(): kv_weight = lax.all_gather(cca_kv, 'seq', axis=0, tiled=True)  28.1 us
    gather x1, local copies, waits for them, and re-layouts, shards(): jnp.take(table, tokens, axis=0).astype(jnp.float32)  17.5 us
    gather x1, local copies, waits for them, and re-layouts, shards(): jnp.take(depth_table, depths, axis=0).astype(jnp.float32)  17 us
    all_to_all x1, waiting for transfers between devices, shards(): lax.all_to_all(embedded, 'tp', split_axis=0, concat_axis=2, tiled=True)  14.1 us
    all_gather x1, waiting for transfers between devices, shards(): encoded = lax.all_gather(encoded_part, 'tp', axis=0, tiled=True)  11.2 us
    unnamed x39, local copies, waits for them, and re-layouts  8.07 us
  transfers between devices with their start and end apart: 9, of which 5 were waited for; matrix products, arithmetic and copies ran while one was open for 25% of the time, Pallas kernels for 0%

commit v1 on v0

v1 whole, which is shorter than its diff:
```python
import functools
import math

import jax
import jax.numpy as jnp
from jax import lax
from jax.experimental import pallas as pl
from jax.experimental.pallas import tpu as pltpu
from jax.sharding import PartitionSpec as P

HD = 128
SCALE = 1.0 / math.sqrt(HD)
MESH = pl.DeviceIdType.MESH
PARTS = ((0, 3), (3, 2))
NT = (((1,), (1,)), ((), ()))


def enter(peers):
    barrier = pltpu.get_barrier_semaphore()
    for peer in peers:
        pl.semaphore_signal(barrier, inc=1, device_id=peer, device_id_type=MESH)
    pl.semaphore_wait(barrier, len(peers))


def gather_kernel(
    seq_size,
    tp_size,
    req_ref,
    tok_ref,
    dep_ref,
    par_ref,
    w_ref,
    cond_ref,
    full_ref,
    resp_ref,
    cond_out,
    asked,
    answer,
    w_send,
    w_recv,
    own_sem,
    q_send,
    q_recv,
    r_send,
    r_recv,
    c_send,
    c_recv,
):
    s, t = lax.axis_index("seq"), lax.axis_index("tp")
    deep = seq_size // 2
    rows = w_ref.shape[1]
    seq_peers = [(lax.rem(s + j, seq_size), t) for j in range(1, seq_size)]
    tp_peers = [(s, lax.rem(t + j, tp_size)) for j in range(1, tp_size)]
    enter(seq_peers + tp_peers)

    started = []
    requests = []
    for j in range(1, seq_size):
        peer = seq_peers[j - 1]
        copy = pltpu.make_async_remote_copy(
            req_ref.at[peer[0]], asked.at[s], q_send.at[j], q_recv.at[seq_size - j], peer, MESH
        )
        copy.start()
        requests.append(copy)

    a, b = s // 2, s % 2
    c, d = t // 2, t % 2

    def place(slot):
        k, fb, fc, fd = slot
        sa = lax.rem(a + k, deep)
        sb = 1 - b if fb else b
        sc = 1 - c if fc else c
        sd = 1 - d if fd else d
        return sa * 2 + sb, sc * 2 + sd

    def landing(part, slot):
        ps, pt = place(slot)
        first, count = PARTS[part]
        return full_ref.at[
            pt, pl.ds(first, count), pl.ds(pl.multiple_of(ps * rows, rows), rows), :
        ]

    def own(part):
        first, count = PARTS[part]
        return w_ref.at[pl.ds(first, count)]

    def send(part, slot, way, hop=0):
        k, fb, fc, fd = slot
        if way == "a":
            peer = (lax.rem(a + hop, deep) * 2 + b, t)
            index = ((deep - hop) % deep, fb, fc, fd)
        elif way == "b":
            peer = (a * 2 + 1 - b, t)
            index = (k, 1, fc, fd)
        elif way == "c":
            peer = (s, (1 - c) * 2 + d)
            index = (k, fb, 1, fd)
        else:
            peer = (s, c * 2 + 1 - d)
            index = (k, fb, fc, 1)
        number = ((index[0] * 2 + index[1]) * 2 + index[2]) * 2 + index[3]
        source = own(part) if slot == (0, 0, 0, 0) else landing(part, slot)
        copy = pltpu.make_async_remote_copy(
            source,
            landing(part, slot),
            w_send.at[part, number],
            w_recv.at[part, number],
            peer,
            MESH,
        )
        copy.start()
        started.append(copy)

    def arrive(part, slot):
        k, fb, fc, fd = slot
        number = ((k * 2 + fb) * 2 + fc) * 2 + fd
        target = landing(part, slot)
        pltpu.make_async_copy(target, target, w_recv.at[part, number]).wait()

    def onward(part, slot):
        k, fb, fc, fd = slot
        if part == 0:
            if not fb and not fc:
                send(part, slot, "b")
            if not fc:
                send(part, slot, "c")
        else:
            if not fb and not fc:
                send(part, slot, "c")
            if not fb:
                send(part, slot, "b")
        send(part, slot, "d")

    for part in range(2):
        for hop in range(1, deep):
            send(part, (0, 0, 0, 0), "a", hop)
    for part in range(2):
        onward(part, (0, 0, 0, 0))
    local = []
    for part in range(2):
        copy = pltpu.make_async_copy(own(part), landing(part, (0, 0, 0, 0)), own_sem.at[part])
        copy.start()
        local.append(copy)
    share = cond_ref.shape[1] // tp_size
    cond_copies = []
    for j in range(1, tp_size):
        peer = tp_peers[j - 1]
        copy = pltpu.make_async_remote_copy(
            cond_ref.at[:, pl.ds(pl.multiple_of(peer[1] * share, share), share), :],
            cond_out.at[t],
            c_send.at[j],
            c_recv.at[tp_size - j],
            peer,
            MESH,
        )
        copy.start()
        cond_copies.append(copy)
    copy = pltpu.make_async_copy(
        cond_ref.at[:, pl.ds(pl.multiple_of(t * share, share), share), :],
        cond_out.at[t],
        own_sem.at[2],
    )
    copy.start()
    local.append(copy)

    asked[s] = req_ref[s]
    for copy in requests:
        copy.wait()
    places = asked[...].reshape(seq_size * 8, 128)[:, :1]
    stored = tok_ref.shape[0]
    pick = (
        lax.broadcasted_iota(jnp.int32, (seq_size * 8, stored), 1) == places
    ).astype(jnp.float32).astype(jnp.bfloat16)

    def chosen(values):
        return jnp.dot(
            pick,
            values.astype(jnp.float32).astype(jnp.bfloat16),
            preferred_element_type=jnp.float32,
        )

    tokens = tok_ref[...]
    high = tokens >> 7
    found = chosen(high) * 128.0 + chosen(tokens - (high << 7))
    answer[:, :, 0:128] = found.astype(jnp.int32).reshape(seq_size, 8, 128)
    answer[:, :, 128:256] = chosen(dep_ref[...]).astype(jnp.int32).reshape(seq_size, 8, 128)
    answer[:, :, 256:384] = chosen(par_ref[...]).astype(jnp.int32).reshape(seq_size, 8, 128)
    answers = []
    for j in range(1, seq_size):
        peer = seq_peers[j - 1]
        copy = pltpu.make_async_remote_copy(
            answer.at[peer[0]], resp_ref.at[s], r_send.at[j], r_recv.at[seq_size - j], peer, MESH
        )
        copy.start()
        answers.append(copy)
    resp_ref[s] = answer[s]

    for step in range(deep + 2):
        for k, group in (
            (step, ((0, 0),)),
            (step - 1, ((1, 0), (0, 1))),
            (step - 2, ((1, 1),)),
        ):
            if 0 <= k < deep:
                for part in range(2):
                    for fb, fc in group if part == 0 else group[::-1]:
                        slot = (k, fb, fc, 0)
                        if slot != (0, 0, 0, 0):
                            arrive(part, slot)
                            onward(part, slot)
    for k in range(deep):
        for fb in range(2):
            for fc in range(2):
                for part in range(2):
                    arrive(part, (k, fb, fc, 1))
    for copy in answers + cond_copies + local:
        copy.wait()
    for copy in started:
        copy.wait_send()


def swap_kernel(tp_size, emb_ref, out_ref, send_sem, recv_sem, own_sem):
    s, t = lax.axis_index("seq"), lax.axis_index("tp")
    share = emb_ref.shape[0] // tp_size
    peers = [(s, lax.rem(t + j, tp_size)) for j in range(1, tp_size)]
    enter(peers)
    copies = []
    for j in range(1, tp_size):
        peer = peers[j - 1]
        copy = pltpu.make_async_remote_copy(
            emb_ref.at[pl.ds(pl.multiple_of(peer[1] * share, share), share), :],
            out_ref.at[t],
            send_sem.at[j],
            recv_sem.at[tp_size - j],
            peer,
            MESH,
        )
        copy.start()
        copies.append(copy)
    copy = pltpu.make_async_copy(
        emb_ref.at[pl.ds(pl.multiple_of(t * share, share), share), :], out_ref.at[t], own_sem
    )
    copy.start()
    copy.wait()
    for copy in copies:
        copy.wait()


def spread_kernel(seq_size, tp_size, kv_ref, out_ref, send_sem, recv_sem, carry_send, carry_recv, own_sem):
    s, t = lax.axis_index("seq"), lax.axis_index("tp")
    share = kv_ref.shape[1]
    lead = out_ref.shape[0] - share * tp_size
    gives = jnp.logical_and(t == tp_size - 1, s < seq_size - 1)
    takes = s > 0
    peers = [(s, lax.rem(t + j, tp_size)) for j in range(1, tp_size)]
    barrier = pltpu.get_barrier_semaphore()
    for peer in peers:
        pl.semaphore_signal(barrier, inc=1, device_id=peer, device_id_type=MESH)

    @pl.when(takes)
    def _():
        pl.semaphore_signal(
            barrier, inc=1, device_id=(s - 1, jnp.int32(tp_size - 1)), device_id_type=MESH
        )

    @pl.when(gives)
    def _():
        pl.semaphore_wait(barrier, 2 * tp_size - 1)

    @pl.when(jnp.logical_not(gives))
    def _():
        pl.semaphore_wait(barrier, tp_size - 1)

    def mine():
        return out_ref.at[pl.ds(pl.multiple_of(lead + t * share, lead), share), :]

    copies = []
    for j in range(1, tp_size):
        peer = peers[j - 1]
        copy = pltpu.make_async_remote_copy(
            kv_ref.at[peer[1]], mine(), send_sem.at[j], recv_sem.at[tp_size - j], peer, MESH
        )
        copy.start()
        copies.append(copy)

    def carry(p):
        return pltpu.make_async_remote_copy(
            kv_ref.at[p, pl.ds(share - lead, lead), :],
            out_ref.at[pl.ds(0, lead), :],
            carry_send.at[p],
            carry_recv,
            (s + 1, jnp.int32(p)),
            MESH,
        )

    @pl.when(gives)
    def _():
        for p in range(tp_size):
            carry(p).start()

    copy = pltpu.make_async_copy(kv_ref.at[t], mine(), own_sem)
    copy.start()
    copy.wait()
    for copy in copies:
        copy.wait()

    @pl.when(gives)
    def _():
        for p in range(tp_size):
            carry(p).wait_send()

    @pl.when(takes)
    def _():
        target = out_ref.at[pl.ds(0, lead), :]
        pltpu.make_async_copy(target, target, carry_recv).wait()


def encoder_kernel(
    tp_size, length, pairs, bias_ref, emb_ref, gain_ref, w_ref, cca_ref, cond_ref, hit_ref, kv_ref, normed, total, q_s, k_s, v_s, mixed
):
    step = pl.program_id(0)
    rows, width = normed.shape
    part = width // tp_size
    blocks = cond_ref.shape[2]
    cond_len = cond_ref.shape[3]

    @pl.when(step == 0)
    def _():
        square = jnp.zeros((rows, 1), jnp.float32)
        for p in range(tp_size):
            piece = emb_ref[p].astype(jnp.float32)
            square += jnp.sum(piece * piece, axis=-1, keepdims=True)
        factor = lax.rsqrt(square * (1.0 / width) + 1e-05)
        for p in range(tp_size):
            columns = slice(p * part, (p + 1) * part)
            normed[:, columns] = (
                emb_ref[p].astype(jnp.float32) * factor * gain_ref[:, columns]
            ).astype(jnp.bfloat16)
            total[:, columns] = emb_ref[p].astype(jnp.float32)

    hidden = normed[...]
    for m, target in ((0, q_s), (1, k_s), (2, v_s)):
        target[...] = jnp.dot(
            hidden, w_ref[0, m], preferred_element_type=jnp.float32
        ).astype(jnp.bfloat16)
    for h in range(part // HD):
        columns = slice(h * HD, (h + 1) * HD)
        bias = bias_ref[step * (part // HD) + h]
        for c in range(blocks):
            cond_k = cond_ref[0, 0, c, :, columns]
            cond_v = cond_ref[0, 1, c, :, columns]
            for k in range(pairs):
                unit = c * pairs + k
                span = slice(unit * length, (unit + 1) * length)
                query = q_s[span, columns]
                near = lax.dot_general(
                    query, k_s[span, columns], NT, preferred_element_type=jnp.float32
                ) * SCALE + bias * hit_ref[unit]
                far = lax.dot_general(
                    query, cond_k, NT, preferred_element_type=jnp.float32
                ) * SCALE
                top = jnp.maximum(
                    jnp.max(near, axis=-1, keepdims=True), jnp.max(far, axis=-1, keepdims=True)
                )
                near, far = jnp.exp(near - top), jnp.exp(far - top)
                share = 1.0 / (
                    jnp.sum(near, axis=-1, keepdims=True) + jnp.sum(far, axis=-1, keepdims=True)
                )
                result = jnp.dot(
                    (near * share).astype(jnp.bfloat16),
                    v_s[span, columns],
                    preferred_element_type=jnp.float32,
                ) + jnp.dot(
                    (far * share).astype(jnp.bfloat16), cond_v, preferred_element_type=jnp.float32
                )
                mixed[span, columns] = result.astype(jnp.bfloat16)
    total[...] += lax.dot_general(
        mixed[...], w_ref[0, 3], NT, preferred_element_type=jnp.float32
    )

    @pl.when(step == tp_size - 1)
    def _():
        encoded = total[...].astype(jnp.bfloat16)
        for p in range(tp_size):
            kv_ref[p] = jnp.dot(
                encoded, cca_ref[p, 0], preferred_element_type=jnp.float32
            ).astype(jnp.bfloat16)


def softmax_rows(scores):
    scores = jnp.exp(scores - jnp.max(scores, axis=-1, keepdims=True))
    return (scores * (1.0 / jnp.sum(scores, axis=-1, keepdims=True))).astype(jnp.bfloat16)


def attend_kernel(allowed_ref, q_ref, prev_ref, cur_ref, out_ref):
    block = pl.program_id(0)
    tokens = q_ref.shape[0]
    heads = q_ref.shape[1] // HD
    query = q_ref[...]
    stacked = jnp.concatenate([query[:, h * HD : (h + 1) * HD] for h in range(heads)], axis=0)
    ok = allowed_ref[block] > 0

    def mix(rows, kv_ref):
        scores = lax.dot_general(
            rows, kv_ref[:, :HD], NT, preferred_element_type=jnp.float32
        ) * SCALE
        return jnp.dot(
            softmax_rows(scores), kv_ref[:, HD:], preferred_element_type=jnp.float32
        )

    leading = mix(stacked, prev_ref)
    tail = query[tokens - 16 :, :]
    tails = jnp.concatenate([tail[:, h * HD : (h + 1) * HD] for h in range(heads)], axis=0)
    trailing = mix(tails, cur_ref)
    last = lax.broadcasted_iota(jnp.int32, (16, HD), 0) == 15
    for h in range(heads):
        columns = slice(h * HD, (h + 1) * HD)
        value = leading[h * tokens : (h + 1) * tokens]
        value = jnp.where(ok, value, jnp.zeros_like(value))
        out_ref[: tokens - 16, columns] = value[: tokens - 16].astype(jnp.bfloat16)
        out_ref[tokens - 16 :, columns] = jnp.where(
            last, trailing[h * 16 : (h + 1) * 16], value[tokens - 16 :]
        ).astype(jnp.bfloat16)


def shards(
    db_tokens,
    db_parent,
    db_depth,
    nb_rows,
    seq_start,
    table,
    depth_table,
    enc_gain,
    enc_qkv,
    tree_bias,
    enc_wo,
    cond_kv,
    queries,
    cca_kv,
):
    seq_size = lax.axis_size("seq")
    tp_size = lax.axis_size("tp")
    block_count, pair_count = nb_rows.shape
    unit_count = block_count * pair_count
    stored, length = db_tokens.shape
    slot_count = max(1, 2 * unit_count // seq_size)
    part = enc_qkv.shape[2]
    rows = enc_qkv.shape[0]
    width = part * tp_size
    cond_len = cond_kv.shape[0] // block_count
    bf16 = jnp.bfloat16
    anywhere = pl.BlockSpec(memory_space=pl.ANY)
    vmem = pl.BlockSpec(memory_space=pltpu.VMEM)
    dma = pltpu.SemaphoreType.DMA

    flat_rows = nb_rows.reshape(unit_count)
    holder = flat_rows // stored
    local_row = flat_rows % stored
    ordering = jnp.arange(unit_count, dtype=jnp.int32)
    earlier = jnp.sum(
        ((holder[:, None] == holder[None, :]) & (ordering[:, None] > ordering[None, :])).astype(
            jnp.int32
        ),
        axis=1,
    )
    target = holder * 8 + earlier
    places = jnp.arange(seq_size * 8, dtype=jnp.int32)
    request = jnp.sum(
        jnp.where(target[None, :] == places[:, None], local_row[None, :], 0), axis=1
    )
    request = jnp.broadcast_to(request.reshape(seq_size, 8, 1), (seq_size, 8, 128))
    packed = jnp.concatenate(
        [
            enc_qkv.transpose(1, 0, 2),
            enc_wo.T[None],
            cca_kv.reshape(1, rows, part),
        ],
        axis=0,
    )
    cond = cond_kv.transpose(1, 0, 2)
    share = unit_count // tp_size
    block_share = block_count // tp_size
    full, response, own_cond = pl.pallas_call(
        functools.partial(gather_kernel, seq_size, tp_size),
        out_shape=(
            jax.ShapeDtypeStruct((tp_size, 5, width, part), bf16),
            jax.ShapeDtypeStruct((seq_size, 8, 384), jnp.int32),
            jax.ShapeDtypeStruct((tp_size, 2, block_share * cond_len, part), bf16),
        ),
        in_specs=[vmem] * 4 + [anywhere] * 2,
        out_specs=(anywhere, vmem, anywhere),
        scratch_shapes=[
            pltpu.VMEM((seq_size, 8, 128), jnp.int32),
            pltpu.VMEM((seq_size, 8, 384), jnp.int32),
            dma((2, seq_size * tp_size)),
            dma((2, seq_size * tp_size)),
            dma((3,)),
            dma((seq_size,)),
            dma((seq_size,)),
            dma((seq_size,)),
            dma((seq_size,)),
            dma((tp_size,)),
            dma((tp_size,)),
        ],
        compiler_params=pltpu.CompilerParams(
            collective_id=0, has_side_effects=True, vmem_limit_bytes=32 << 20
        ),
        name="gather_weights_and_rows",
    )(request, db_tokens, db_depth, db_parent, packed, cond)

    answer = jnp.take(response.reshape(seq_size * 8, 384), target, axis=0, mode="clip")
    tokens = answer[:, :length].reshape(unit_count * length)
    depths = answer[:, length : 2 * length].reshape(unit_count * length)
    parents = lax.dynamic_slice_in_dim(
        answer[:, 2 * length :], lax.axis_index("tp") * share, share, 0
    )
    hit = (parents[:, :, None] == jnp.arange(length, dtype=jnp.int32)).astype(jnp.float32)
    depth_pick = (
        depths[:, None] == jnp.arange(depth_table.shape[0], dtype=jnp.int32)[None, :]
    ).astype(bf16)
    embedded = (
        jnp.take(table, tokens, axis=0, mode="clip").astype(jnp.float32)
        + jnp.dot(depth_pick, depth_table, preferred_element_type=jnp.float32)
    ).astype(bf16)

    mine = share * length
    own_emb = pl.pallas_call(
        functools.partial(swap_kernel, tp_size),
        out_shape=jax.ShapeDtypeStruct((tp_size, mine, part), bf16),
        in_specs=[anywhere],
        out_specs=anywhere,
        scratch_shapes=[dma((tp_size,)), dma((tp_size,)), dma],
        compiler_params=pltpu.CompilerParams(collective_id=1, has_side_effects=True),
        name="swap_embedded_columns",
    )(embedded)

    cond_blocks = own_cond.reshape(tp_size, 2, block_share, cond_len, part)
    keys_values = pl.pallas_call(
        functools.partial(encoder_kernel, tp_size, length, pair_count),
        grid=(tp_size,),
        out_shape=jax.ShapeDtypeStruct((tp_size, mine, part), bf16),
        in_specs=[
            pl.BlockSpec(memory_space=pltpu.SMEM),
            pl.BlockSpec((tp_size, mine, part), lambda i: (0, 0, 0)),
            pl.BlockSpec((1, width), lambda i: (0, 0)),
            pl.BlockSpec((1, 4, width, part), lambda i: (i, 0, 0, 0)),
            pl.BlockSpec((tp_size, 1, width, part), lambda i: (0, 4, 0, 0)),
            pl.BlockSpec((1, 2, block_share, cond_len, part), lambda i: (i, 0, 0, 0, 0)),
            pl.BlockSpec((share, length, length), lambda i: (0, 0, 0)),
        ],
        out_specs=pl.BlockSpec((tp_size, mine, part), lambda i: (0, 0, 0)),
        scratch_shapes=[
            pltpu.VMEM((mine, width), bf16),
            pltpu.VMEM((mine, width), jnp.float32),
            pltpu.VMEM((mine, part), bf16),
            pltpu.VMEM((mine, part), bf16),
            pltpu.VMEM((mine, part), bf16),
            pltpu.VMEM((mine, part), bf16),
        ],
        compiler_params=pltpu.CompilerParams(vmem_limit_bytes=48 << 20),
        name="encode",
    )(tree_bias, own_emb, enc_gain.reshape(1, width), full, full, cond_blocks, hit)

    key_rows = pair_count * length
    spread = pl.pallas_call(
        functools.partial(spread_kernel, seq_size, tp_size),
        out_shape=jax.ShapeDtypeStruct(((block_count + 1) * key_rows, part), bf16),
        in_specs=[anywhere],
        out_specs=anywhere,
        scratch_shapes=[dma((tp_size,)), dma((tp_size,)), dma((tp_size,)), dma, dma],
        compiler_params=pltpu.CompilerParams(collective_id=2, has_side_effects=True),
        name="spread_keys_values",
    )(keys_values)

    block_index = lax.axis_index("seq") * block_count + jnp.arange(block_count, dtype=jnp.int32)
    allowed = ((block_index > 0) & (seq_start == 0)).astype(jnp.int32)
    columns = queries.shape[1]
    return pl.pallas_call(
        attend_kernel,
        grid=(block_count,),
        out_shape=jax.ShapeDtypeStruct(queries.shape, bf16),
        in_specs=[
            pl.BlockSpec(memory_space=pltpu.SMEM),
            pl.BlockSpec((cond_len, columns), lambda i: (i, 0)),
            pl.BlockSpec((key_rows, part), lambda i: (i, 0)),
            pl.BlockSpec((key_rows, part), lambda i: (i + 1, 0)),
        ],
        out_specs=pl.BlockSpec((cond_len, columns), lambda i: (i, 0)),
        compiler_params=pltpu.CompilerParams(vmem_limit_bytes=32 << 20),
        name="attend",
    )(allowed, queries, spread, spread)


def solution(mesh):
    in_specs = (
        P("seq", None),
        P("seq", None),
        P("seq", None),
        P("seq", None),
        P("seq"),
        P(None, "tp"),
        P(None, "tp"),
        P(),
        P("seq", None, "tp"),
        P(),
        P("tp", "seq"),
        P("seq", None, "tp"),
        P("seq", "tp"),
        P("seq", None, "tp"),
    )
    out_specs = P("seq", "tp")
    return jax.shard_map(shards, mesh=mesh, in_specs=in_specs, out_specs=out_specs, check_vma=False)
```

time: 311 us -> 162 us (0.52)
  Pallas kernels: 0 us -> 134 us
  blocking collectives: 96.9 us -> 0 us
  waiting for transfers between devices: 81.6 us -> 0 us
  local copies, waits for them, and re-layouts: 59.7 us -> 23.1 us
  starting transfers between devices: 24.5 us -> 0 us
  matrix products: 19.6 us -> 1.54 us
  between operations: 13.6 us -> 0.24 us
  other arithmetic: 12.8 us -> 2.15 us
    pallas_call x0 -> x5, Pallas kernels: none -> 134 us  [the longest x1 72.4 us: shards(): pl.pallas_call(functools.partial(gather_kernel, seq_size, tp_size), out_s...]
    all_gather x2 -> x0, blocking collectives: 89.2 us -> none  [the longest x1 61.1 us: shards(): lax.all_gather(enc_wo, 'seq', axis=1, tiled=True)]
    all_gather x4 -> x0, waiting for transfers between devices: 57.6 us -> none  [the longest x1 46.4 us: shards(): lax.all_gather(enc_qkv, 'seq', axis=0, tiled=True)]
    gather x7 -> x2, local copies, waits for them, and re-layouts: 38.4 us -> 11.7 us  [the longest x1 11.1 us: shards(): jnp.take(table, tokens, axis=0, mode='clip').astype(jnp.float32)]
    all_to_all x4 -> x0, starting transfers between devices: 21.3 us -> none  [the longest x1 6.03 us: shards(): lax.all_to_all(cond_flat, 'tp', split_axis=0, concat_axis=2, tiled=True)]
    all_to_all x4 -> x0, waiting for transfers between devices: 20.4 us -> none  [the longest x1 14.1 us: shards(): lax.all_to_all(embedded, 'tp', split_axis=0, concat_axis=2, tiled=True)]
    dot_general x11 -> x1, matrix products: 19.6 us -> 1.54 us  [shards(): jnp.dot(depth_pick, depth_table, preferred_element_type=jnp.float32)]
    convert_element_type x7 -> x2, other arithmetic: 8.57 us -> 0.86 us  [the longest x1 0.73 us: shards(): allowed = ((block_index > 0) & (seq_start == 0)).astype(jnp.int32)]
  transfers between devices with their start and end apart: 9 -> 0, of which waited for: 5 -> 0; matrix products, arithmetic and copies ran while one was open for 25% -> 0% of each run, Pallas kernels for 0% -> 0%
where the time goes in v1:
time: 162 us; the launch traced here: 161 us
  Pallas kernels  134 us (83%)
  local copies, waits for them, and re-layouts  23.1 us (14%)
  other arithmetic  2.15 us (1%)
    pallas_call x1, Pallas kernels, shards(): pl.pallas_call(functools.partial(gather_kernel, seq_size, tp_size), out_s...  72.4 us
    pallas_call x1, Pallas kernels, shards(): pl.pallas_call(functools.partial(encoder_kernel, tp_size, length, pair_co...  22.4 us
    pallas_call x1, Pallas kernels, shards(): pl.pallas_call(functools.partial(spread_kernel, seq_size, tp_size), out_s...  18.4 us
    pallas_call x1, Pallas kernels, shards(): pl.pallas_call(functools.partial(swap_kernel, tp_size), out_shape=jax.Sha...  14.1 us
    gather x1, local copies, waits for them, and re-layouts, shards(): jnp.take(table, tokens, axis=0, mode='clip').astype(jnp.float32)  11.1 us
    unnamed x25, local copies, waits for them, and re-layouts  10.3 us
    pallas_call x1, Pallas kernels, shards(): pl.pallas_call(attend_kernel, grid=(block_count,), out_shape=jax.ShapeDty...  7.11 us

profile of v1, /device:TPU:13, one launch (start us, length us, event | category | flops | bytes accessed | tf_op | source)
XLA Modules:
  0.0 161.5 jit_solution(17592384695469425200)
XLA Ops:
  0.0 0.0 copy-start
  0.0 0.0 copy-start.7
  0.0 0.0 copy-start.8
  0.0 0.0 copy-start.6
  0.0 0.7 and_convert_fusion.allowed_ref
  0.8 0.8 copy.23
  1.5 0.1 reshape.177
  1.6 0.1 reshape.174
  1.7 0.2 convert_reduce_fusion
  1.9 0.1 select_reduce_fusion
  2.0 0.1 broadcast_in_dim.40
  2.1 0.1 broadcast_in_dim.41.req_ref
  2.2 0.9 copy.24
  3.1 0.9 reshape.175
  4.0 1.0 pad_maximum_fusion.w_ref
  5.0 1.1 copy.28
  6.1 0.0 copy-done.7
  6.1 0.0 copy-done.8
  6.1 0.0 copy-done.6
  6.1 72.4 %gather_weights_and_rows.1 = (bf16[4,5,1024,256]{3,2,1,0:T(8,128)(2,1)S(1)}, s32[8,8,384]{2,1,0:T(8,128)S(1)}, bf16[4,2,128,256]{3,2,1,0:T(8,128)(2,1)S(1)}) custom-call(s32[8,8,128]{2,1,0:T(8,128)S(1)} %broadcast_in_dim.41.req_ref, s32[512,128]{1,0:T(8,128)S(1)} %copy-done.6, s32[512,128]{1,0:T(8,128)S(1)} %copy-done.7, s32[512,128]{1,0:T(8,128)S(1)} %copy-done.8, ...), custom_call_target="tpu_custom_call" | custom-call | tf_op jit(solution)/shard_map/gather_weights_and_rows/pallas_call | solution.py:485
  78.6 0.0 copy-start.1
  78.6 4.0 %copy-done.1 = bf16[4,5,1024,256]{3,2,1,0:T(8,128)(2,1)} copy-done((bf16[4,5,1024,256]{3,2,1,0:T(8,128)(2,1)}, bf16[4,5,1024,256]{3,2,1,0:T(8,128)(2,1)S(1)}, u32[]{:S(2)}) %copy-start.1) | copy-done | bytes 10485784
  82.5 0.6 gather_fusion
  83.2 0.1 fusion.2.hit_ref
  83.3 11.1 %gather_fusion.1 = bf16[2048,256]{1,0:T(8,128)(2,1)S(1)} fusion(bf16[16384,256]{1,0:T(8,128)(2,1)} %param.19, s32[2048]{0:T(1024)S(1)} %fusion.3), kind=kCustom, calls=%fused_computation.1 | custom fusion | bytes 2105344 | tf_op jit(solution)/shard_map/jit(_take)/gather | solution.py:524
  94.4 0.0 copy-done
  94.4 0.0 copy-start.9
  94.4 0.0 copy-start.10
  94.4 1.5 fusion.emb_ref
  96.0 14.1 %swap_embedded_columns.1.emb_ref = bf16[4,512,256]{2,1,0:T(8,128)(2,1)} custom-call(bf16[2048,256]{1,0:T(8,128)(2,1)} %fusion.emb_ref), custom_call_target="tpu_custom_call" | custom-call | tf_op jit(solution)/shard_map/swap_embedded_columns/pallas_call | solution.py:529
  110.1 0.0 copy-done.9
  110.1 0.0 copy-done.10
  110.1 0.0 copy-start.3
  110.1 1.2 copy-done.3
  111.3 22.4 %encode.1.kv_ref = bf16[4,512,256]{2,1,0:T(8,128)(2,1)S(1)} custom-call(f32[8]{0:T(128)S(1)} %copy-done.10, bf16[4,512,256]{2,1,0:T(8,128)(2,1)S(1)} %copy-done.3, f32[1,1024]{1,0:T(1,128)S(1)} %bitcast.26, bf16[4,5,1024,256]{3,2,1,0:T(8,128)(2,1)} %copy-done.1, bf16[4,5,1024,256]{3,2,1,0:T(8,128)(2,1)} %copy-done.1, ...), custom_call_target="tpu_custom_call" | custom-call | tf_op jit(solution)/shard_map/encode/pallas_call | solution.py:540
  133.7 0.0 copy-start.4
  133.7 1.0 copy-done.4
  134.7 0.0 copy-start.5
  134.7 18.4 %spread_keys_values.1.prev_ref.cur_ref = bf16[2304,256]{1,0:T(8,128)(2,1)} custom-call(bf16[4,512,256]{2,1,0:T(8,128)(2,1)} %copy-done.4), custom_call_target="tpu_custom_call" | custom-call | tf_op jit(solution)/shard_map/spread_keys_values/pallas_call | solution.py:567
  153.1 0.0 copy-done.5
  153.1 0.0 copy-start.2
  153.1 1.3 copy-done.2
  154.4 7.1 %attend.1 = bf16[512,1024]{1,0:T(8,128)(2,1)} custom-call(s32[8]{0:T(128)S(1)} %and_convert_fusion.allowed_ref, bf16[512,1024]{1,0:T(8,128)(2,1)S(1)} %copy-done.5, bf16[2304,256]{1,0:T(8,128)(2,1)S(1)} %copy-done.2, bf16[2304,256]{1,0:T(8,128)(2,1)S(1)} %copy-done.2), custom_call_target="tpu_custom_call" | custom-call | tf_op jit(solution)/shard_map/attend/pallas_call | solution.py:580
  (7 shorter events, 0.1 us)
Async XLA Ops:
  0.0 94.4 %copy-start = (bf16[32,256]{1,0:T(8,128)(2,1)S(1)}, bf16[32,256]{1,0:T(8,128)(2,1)}, u32[]{:S(2)}) copy-start(bf16[32,256]{1,0:T(8,128)(2,1)} %param.20) | copy-start | bytes 49156
  0.0 6.1 %copy-start.7 = (s32[512,128]{1,0:T(8,128)S(1)}, s32[512,128]{1,0:T(8,128)}, u32[]{:S(2)}) copy-start(s32[512,128]{1,0:T(8,128)} %dep_ref.1) | copy-start | bytes 786436
  0.0 6.1 %copy-start.8 = (s32[512,128]{1,0:T(8,128)S(1)}, s32[512,128]{1,0:T(8,128)}, u32[]{:S(2)}) copy-start(s32[512,128]{1,0:T(8,128)} %par_ref.1) | copy-start | bytes 786436
  0.0 6.1 %copy-start.6 = (s32[512,128]{1,0:T(8,128)S(1)}, s32[512,128]{1,0:T(8,128)}, u32[]{:S(2)}) copy-start(s32[512,128]{1,0:T(8,128)} %tok_ref.1) | copy-start | bytes 786436
  78.6 4.0 %copy-start.1 = (bf16[4,5,1024,256]{3,2,1,0:T(8,128)(2,1)}, bf16[4,5,1024,256]{3,2,1,0:T(8,128)(2,1)S(1)}, u32[]{:S(2)}) copy-start(bf16[4,5,1024,256]{3,2,1,0:T(8,128)(2,1)S(1)} %get-tuple-element.9.w_ref.cca_ref) | copy-start | bytes 31457284
  94.4 15.6 %copy-start.9 = (f32[1024]{0:T(1024)S(1)}, f32[1024]{0:T(1024)}, u32[]{:S(2)}) copy-start(f32[1024]{0:T(1024)} %param.21) | copy-start | bytes 12292
  94.4 15.6 %copy-start.10 = (f32[8]{0:T(128)S(1)}, f32[8]{0:T(128)}, u32[]{:S(2)}) copy-start(f32[8]{0:T(128)} %bias_ref.1) | copy-start | bytes 100
  110.1 1.2 copy-start.3
  133.7 1.0 copy-start.4
  134.7 18.4 %copy-start.5 = (bf16[512,1024]{1,0:T(8,128)(2,1)S(1)}, bf16[512,1024]{1,0:T(8,128)(2,1)}, u32[]{:S(2)}) copy-start(bf16[512,1024]{1,0:T(8,128)(2,1)} %q_ref.1) | copy-start | bytes 3145732
  153.1 1.3 copy-start.2

commit v2 on v1

--- a/solution.py
+++ b/solution.py
@@ -11,7 +11,7 @@
 HD = 128
 SCALE = 1.0 / math.sqrt(HD)
 MESH = pl.DeviceIdType.MESH
-PARTS = ((0, 3), (3, 2))
+PARTS = ((0, 2), (2, 3))
 NT = (((1,), (1,)), ((), ()))
 
 
@@ -22,29 +22,92 @@
     pl.semaphore_wait(barrier, len(peers))
 
 
+def fetch_kernel(
+    seq_size, tp_size, req_ref, tok_ref, dep_ref, par_ref, cond_ref, resp_ref, cond_out, asked, answer, own_sem, q_send, q_recv, r_send, r_recv, c_send, c_recv
+):
+    s, t = lax.axis_index("seq"), lax.axis_index("tp")
+    seq_peers = [(lax.rem(s + j, seq_size), t) for j in range(1, seq_size)]
+    tp_peers = [(s, lax.rem(t + j, tp_size)) for j in range(1, tp_size)]
+    enter(seq_peers + tp_peers)
+    requests = []
+    for j in range(1, seq_size):
+        peer = seq_peers[j - 1]
+        copy = pltpu.make_async_remote_copy(
+            req_ref.at[peer[0]], asked.at[s], q_send.at[j], q_recv.at[seq_size - j], peer, MESH
+        )
+        copy.start()
+        requests.append(copy)
+
+    share = cond_ref.shape[1] // tp_size
+    cond_copies = []
+    for j in range(1, tp_size):
+        peer = tp_peers[j - 1]
+        copy = pltpu.make_async_remote_copy(
+            cond_ref.at[:, pl.ds(pl.multiple_of(peer[1] * share, share), share), :],
+            cond_out.at[t],
+            c_send.at[j],
+            c_recv.at[tp_size - j],
+            peer,
+            MESH,
+        )
+        copy.start()
+        cond_copies.append(copy)
+    copy = pltpu.make_async_copy(
+        cond_ref.at[:, pl.ds(pl.multiple_of(t * share, share), share), :],
+        cond_out.at[t],
+        own_sem,
+    )
+    copy.start()
+    kept = copy
+
+    asked[s] = req_ref[s]
+    for copy in requests:
+        copy.wait()
+    places = asked[...].reshape(seq_size * 8, 128)[:, :1]
+    stored = tok_ref.shape[0]
+    pick = (
+        lax.broadcasted_iota(jnp.int32, (seq_size * 8, stored), 1) == places
+    ).astype(jnp.float32).astype(jnp.bfloat16)
+
+    def chosen(values):
+        return jnp.dot(
+            pick,
+            values.astype(jnp.float32).astype(jnp.bfloat16),
+            preferred_element_type=jnp.float32,
+        )
+
+    tokens = tok_ref[...]
+    high = tokens >> 7
+    found = chosen(high) * 128.0 + chosen(tokens - (high << 7))
+    answer[:, :, 0:128] = found.astype(jnp.int32).reshape(seq_size, 8, 128)
+    answer[:, :, 128:256] = chosen(dep_ref[...]).astype(jnp.int32).reshape(seq_size, 8, 128)
+    answer[:, :, 256:384] = chosen(par_ref[...]).astype(jnp.int32).reshape(seq_size, 8, 128)
+    answers = []
+    for j in range(1, seq_size):
+        peer = seq_peers[j - 1]
+        copy = pltpu.make_async_remote_copy(
+            answer.at[peer[0]], resp_ref.at[s], r_send.at[j], r_recv.at[seq_size - j], peer, MESH
+        )
+        copy.start()
+        answers.append(copy)
+    resp_ref[s] = answer[s]
+
+    for copy in answers + cond_copies + [kept]:
+        copy.wait()
+
+
 def gather_kernel(
     seq_size,
     tp_size,
-    req_ref,
-    tok_ref,
-    dep_ref,
-    par_ref,
     w_ref,
-    cond_ref,
+    emb_ref,
     full_ref,
-    resp_ref,
-    cond_out,
-    asked,
-    answer,
+    emb_out,
     w_send,
     w_recv,
     own_sem,
-    q_send,
-    q_recv,
-    r_send,
-    r_recv,
-    c_send,
-    c_recv,
+    e_send,
+    e_recv,
 ):
     s, t = lax.axis_index("seq"), lax.axis_index("tp")
     deep = seq_size // 2
@@ -54,15 +117,6 @@
     enter(seq_peers + tp_peers)
 
     started = []
-    requests = []
-    for j in range(1, seq_size):
-        peer = seq_peers[j - 1]
-        copy = pltpu.make_async_remote_copy(
-            req_ref.at[peer[0]], asked.at[s], q_send.at[j], q_recv.at[seq_size - j], peer, MESH
-        )
-        copy.start()
-        requests.append(copy)
-
     a, b = s // 2, s % 2
     c, d = t // 2, t % 2
 
@@ -142,59 +196,27 @@
         copy = pltpu.make_async_copy(own(part), landing(part, (0, 0, 0, 0)), own_sem.at[part])
         copy.start()
         local.append(copy)
-    share = cond_ref.shape[1] // tp_size
-    cond_copies = []
+    share = emb_ref.shape[0] // tp_size
+    emb_copies = []
     for j in range(1, tp_size):
         peer = tp_peers[j - 1]
         copy = pltpu.make_async_remote_copy(
-            cond_ref.at[:, pl.ds(pl.multiple_of(peer[1] * share, share), share), :],
-            cond_out.at[t],
-            c_send.at[j],
-            c_recv.at[tp_size - j],
+            emb_ref.at[pl.ds(pl.multiple_of(peer[1] * share, share), share), :],
+            emb_out.at[t],
+            e_send.at[j],
+            e_recv.at[tp_size - j],
             peer,
             MESH,
         )
         copy.start()
-        cond_copies.append(copy)
+        emb_copies.append(copy)
     copy = pltpu.make_async_copy(
-        cond_ref.at[:, pl.ds(pl.multiple_of(t * share, share), share), :],
-        cond_out.at[t],
+        emb_ref.at[pl.ds(pl.multiple_of(t * share, share), share), :],
+        emb_out.at[t],
         own_sem.at[2],
     )
     copy.start()
     local.append(copy)
-
-    asked[s] = req_ref[s]
-    for copy in requests:
-        copy.wait()
-    places = asked[...].reshape(seq_size * 8, 128)[:, :1]
-    stored = tok_ref.shape[0]
-    pick = (
-        lax.broadcasted_iota(jnp.int32, (seq_size * 8, stored), 1) == places
-    ).astype(jnp.float32).astype(jnp.bfloat16)
-
-    def chosen(values):
-        return jnp.dot(
-            pick,
-            values.astype(jnp.float32).astype(jnp.bfloat16),
-            preferred_element_type=jnp.float32,
-        )
-
-    tokens = tok_ref[...]
-    high = tokens >> 7
-    found = chosen(high) * 128.0 + chosen(tokens - (high << 7))
-    answer[:, :, 0:128] = found.astype(jnp.int32).reshape(seq_size, 8, 128)
-    answer[:, :, 128:256] = chosen(dep_ref[...]).astype(jnp.int32).reshape(seq_size, 8, 128)
-    answer[:, :, 256:384] = chosen(par_ref[...]).astype(jnp.int32).reshape(seq_size, 8, 128)
-    answers = []
-    for j in range(1, seq_size):
-        peer = seq_peers[j - 1]
-        copy = pltpu.make_async_remote_copy(
-            answer.at[peer[0]], resp_ref.at[s], r_send.at[j], r_recv.at[seq_size - j], peer, MESH
-        )
-        copy.start()
-        answers.append(copy)
-    resp_ref[s] = answer[s]
 
     for step in range(deep + 2):
         for k, group in (
@@ -214,37 +236,10 @@
             for fc in range(2):
                 for part in range(2):
                     arrive(part, (k, fb, fc, 1))
-    for copy in answers + cond_copies + local:
+    for copy in emb_copies + local:
         copy.wait()
     for copy in started:
         copy.wait_send()
-
-
-def swap_kernel(tp_size, emb_ref, out_ref, send_sem, recv_sem, own_sem):
-    s, t = lax.axis_index("seq"), lax.axis_index("tp")
-    share = emb_ref.shape[0] // tp_size
-    peers = [(s, lax.rem(t + j, tp_size)) for j in range(1, tp_size)]
-    enter(peers)
-    copies = []
-    for j in range(1, tp_size):
-        peer = peers[j - 1]
-        copy = pltpu.make_async_remote_copy(
-            emb_ref.at[pl.ds(pl.multiple_of(peer[1] * share, share), share), :],
-            out_ref.at[t],
-            send_sem.at[j],
-            recv_sem.at[tp_size - j],
-            peer,
-            MESH,
-        )
-        copy.start()
-        copies.append(copy)
-    copy = pltpu.make_async_copy(
-        emb_ref.at[pl.ds(pl.multiple_of(t * share, share), share), :], out_ref.at[t], own_sem
-    )
-    copy.start()
-    copy.wait()
-    for copy in copies:
-        copy.wait()
 
 
 def spread_kernel(seq_size, tp_size, kv_ref, out_ref, send_sem, recv_sem, carry_send, carry_recv, own_sem):
@@ -344,37 +339,55 @@
         target[...] = jnp.dot(
             hidden, w_ref[0, m], preferred_element_type=jnp.float32
         ).astype(jnp.bfloat16)
-    for h in range(part // HD):
-        columns = slice(h * HD, (h + 1) * HD)
+    jobs = [
+        (h, c, c * pairs + k)
+        for h in range(part // HD)
+        for c in range(blocks)
+        for k in range(pairs)
+    ]
+
+    def span_of(h, unit):
+        return slice(unit * length, (unit + 1) * length), slice(h * HD, (h + 1) * HD)
+
+    scores = []
+    for h, c, unit in jobs:
+        span, columns = span_of(h, unit)
+        query = q_s[span, columns]
+        near = lax.dot_general(query, k_s[span, columns], NT, preferred_element_type=jnp.float32)
+        far = lax.dot_general(
+            query, cond_ref[0, 0, c, :, columns], NT, preferred_element_type=jnp.float32
+        )
         bias = bias_ref[step * (part // HD) + h]
-        for c in range(blocks):
-            cond_k = cond_ref[0, 0, c, :, columns]
-            cond_v = cond_ref[0, 1, c, :, columns]
-            for k in range(pairs):
-                unit = c * pairs + k
-                span = slice(unit * length, (unit + 1) * length)
-                query = q_s[span, columns]
-                near = lax.dot_general(
-                    query, k_s[span, columns], NT, preferred_element_type=jnp.float32
-                ) * SCALE + bias * hit_ref[unit]
-                far = lax.dot_general(
-                    query, cond_k, NT, preferred_element_type=jnp.float32
-                ) * SCALE
-                top = jnp.maximum(
-                    jnp.max(near, axis=-1, keepdims=True), jnp.max(far, axis=-1, keepdims=True)
-                )
-                near, far = jnp.exp(near - top), jnp.exp(far - top)
-                share = 1.0 / (
-                    jnp.sum(near, axis=-1, keepdims=True) + jnp.sum(far, axis=-1, keepdims=True)
-                )
-                result = jnp.dot(
-                    (near * share).astype(jnp.bfloat16),
-                    v_s[span, columns],
-                    preferred_element_type=jnp.float32,
-                ) + jnp.dot(
-                    (far * share).astype(jnp.bfloat16), cond_v, preferred_element_type=jnp.float32
-                )
-                mixed[span, columns] = result.astype(jnp.bfloat16)
+        scores.append((near * SCALE + bias * hit_ref[unit], far * SCALE))
+    tops = [
+        jnp.maximum(
+            jnp.max(near, axis=-1, keepdims=True), jnp.max(far, axis=-1, keepdims=True)
+        )
+        for near, far in scores
+    ]
+    scores = [(jnp.exp(near - top), jnp.exp(far - top)) for (near, far), top in zip(scores, tops)]
+    shares = [
+        1.0 / (jnp.sum(near, axis=-1, keepdims=True) + jnp.sum(far, axis=-1, keepdims=True))
+        for near, far in scores
+    ]
+    results = []
+    for (h, c, unit), (near, far), share in zip(jobs, scores, shares):
+        span, columns = span_of(h, unit)
+        results.append(
+            jnp.dot(
+                (near * share).astype(jnp.bfloat16),
+                v_s[span, columns],
+                preferred_element_type=jnp.float32,
+            )
+            + jnp.dot(
+                (far * share).astype(jnp.bfloat16),
+                cond_ref[0, 1, c, :, columns],
+                preferred_element_type=jnp.float32,
+            )
+        )
+    for (h, c, unit), result in zip(jobs, results):
+        span, columns = span_of(h, unit)
+        mixed[span, columns] = result.astype(jnp.bfloat16)
     total[...] += lax.dot_general(
         mixed[...], w_ref[0, 3], NT, preferred_element_type=jnp.float32
     )
@@ -482,21 +495,18 @@
     cond = cond_kv.transpose(1, 0, 2)
     share = unit_count // tp_size
     block_share = block_count // tp_size
-    full, response, own_cond = pl.pallas_call(
-        functools.partial(gather_kernel, seq_size, tp_size),
+    response, own_cond = pl.pallas_call(
+        functools.partial(fetch_kernel, seq_size, tp_size),
         out_shape=(
-            jax.ShapeDtypeStruct((tp_size, 5, width, part), bf16),
             jax.ShapeDtypeStruct((seq_size, 8, 384), jnp.int32),
             jax.ShapeDtypeStruct((tp_size, 2, block_share * cond_len, part), bf16),
         ),
-        in_specs=[vmem] * 4 + [anywhere] * 2,
-        out_specs=(anywhere, vmem, anywhere),
+        in_specs=[vmem] * 4 + [anywhere],
+        out_specs=(vmem, anywhere),
         scratch_shapes=[
             pltpu.VMEM((seq_size, 8, 128), jnp.int32),
             pltpu.VMEM((seq_size, 8, 384), jnp.int32),
-            dma((2, seq_size * tp_size)),
-            dma((2, seq_size * tp_size)),
-            dma((3,)),
+            dma,
             dma((seq_size,)),
             dma((seq_size,)),
             dma((seq_size,)),
@@ -505,10 +515,10 @@
             dma((tp_size,)),
         ],
         compiler_params=pltpu.CompilerParams(
-            collective_id=0, has_side_effects=True, vmem_limit_bytes=32 << 20
+            collective_id=0, has_side_effects=True, vmem_limit_bytes=12 << 20
         ),
-        name="gather_weights_and_rows",
-    )(request, db_tokens, db_depth, db_parent, packed, cond)
+        name="fetch_rows",
+    )(request, db_tokens, db_depth, db_parent, cond)
 
     answer = jnp.take(response.reshape(seq_size * 8, 384), target, axis=0, mode="clip")
     tokens = answer[:, :length].reshape(unit_count * length)
@@ -526,15 +536,24 @@
     ).astype(bf16)
 
     mine = share * length
-    own_emb = pl.pallas_call(
-        functools.partial(swap_kernel, tp_size),
-        out_shape=jax.ShapeDtypeStruct((tp_size, mine, part), bf16),
-        in_specs=[anywhere],
-        out_specs=anywhere,
-        scratch_shapes=[dma((tp_size,)), dma((tp_size,)), dma],
+    full, own_emb = pl.pallas_call(
+        functools.partial(gather_kernel, seq_size, tp_size),
+        out_shape=(
+            jax.ShapeDtypeStruct((tp_size, 5, width, part), bf16),
+            jax.ShapeDtypeStruct((tp_size, mine, part), bf16),
+        ),
+        in_specs=[anywhere] * 2,
+        out_specs=(anywhere, anywhere),
+        scratch_shapes=[
+            dma((2, seq_size * tp_size)),
+            dma((2, seq_size * tp_size)),
+            dma((3,)),
+            dma((tp_size,)),
+            dma((tp_size,)),
+        ],
         compiler_params=pltpu.CompilerParams(collective_id=1, has_side_effects=True),
-        name="swap_embedded_columns",
-    )(embedded)
+        name="gather_weights_and_embedded",
+    )(packed, embedded)
 
     cond_blocks = own_cond.reshape(tp_size, 2, block_share, cond_len, part)
     keys_values = pl.pallas_call(

time: 162 us -> 145 us (0.90)
  Pallas kernels: 134 us -> 121 us
  local copies, waits for them, and re-layouts: 23.1 us -> 20.4 us
    pallas_call x1, Pallas kernels: 22.4 us -> 12.2 us  [shards(): pl.pallas_call(functools.partial(encoder_kernel, tp_size, length, pair_co...]
    pallas_call x1, Pallas kernels: 14.1 us -> 10.8 us  [shards(): pl.pallas_call(functools.partial(fetch_kernel, seq_size, tp_size), out_sh...]
    unnamed x25 -> x31, local copies, waits for them, and re-layouts: 10.3 us -> 8.33 us
where the time goes in v2:
time: 145 us; the launch traced here: 144 us
  Pallas kernels  121 us (83%)
  local copies, waits for them, and re-layouts  20.4 us (14%)
  matrix products  1.53 us (1%)
    pallas_call x1, Pallas kernels, shards(): pl.pallas_call(functools.partial(gather_kernel, seq_size, tp_size), out_s...  73.8 us
    pallas_call x1, Pallas kernels, shards(): pl.pallas_call(functools.partial(spread_kernel, seq_size, tp_size), out_s...  16.9 us
    pallas_call x1, Pallas kernels, shards(): pl.pallas_call(functools.partial(encoder_kernel, tp_size, length, pair_co...  12.2 us
    gather x1, local copies, waits for them, and re-layouts, shards(): jnp.take(table, tokens, axis=0, mode='clip').astype(jnp.float32)  11.1 us
    pallas_call x1, Pallas kernels, shards(): pl.pallas_call(functools.partial(fetch_kernel, seq_size, tp_size), out_sh...  10.8 us
    unnamed x31, local copies, waits for them, and re-layouts  8.33 us
    pallas_call x1, Pallas kernels, shards(): pl.pallas_call(attend_kernel, grid=(block_count,), out_shape=jax.ShapeDty...  7.11 us

profile of v2, /device:TPU:13, one launch (start us, length us, event | category | flops | bytes accessed | tf_op | source)
XLA Modules:
  0.0 144.2 jit_solution(1942435014162348506)
XLA Ops:
  0.0 0.0 copy-start
  0.0 0.8 copy.24
  0.8 0.1 reshape.175
  0.9 0.2 convert_reduce_fusion
  1.1 0.1 select_reduce_fusion
  1.1 0.1 broadcast_in_dim.41
  1.2 0.1 broadcast_in_dim.42.req_ref
  1.3 1.1 copy.28
  2.4 0.0 copy-start.5
  2.4 0.9 copy-done.5
  3.4 0.0 copy-start.6
  3.4 0.9 copy-done.6
  4.3 0.0 copy-start.7
  4.3 0.9 copy-done.7
  5.3 10.8 %fetch_rows.1 = (s32[8,8,384]{2,1,0:T(8,128)S(1)}, bf16[4,2,128,256]{3,2,1,0:T(8,128)(2,1)S(1)}) custom-call(s32[8,8,128]{2,1,0:T(8,128)S(1)} %broadcast_in_dim.42.req_ref, s32[512,128]{1,0:T(8,128)S(1)} %copy-done.5, s32[512,128]{1,0:T(8,128)S(1)} %copy-done.6, s32[512,128]{1,0:T(8,128)S(1)} %copy-done.7, bf16[2,512,256]{2,1,0:T(8,128)(2,1)S(1)} %bitcast.23), custom_call_target="tpu_custom_call" | custom-call | tf_op jit(solution)/shard_map/fetch_rows/pallas_call | solution.py:498
  16.0 0.1 reshape.177
  16.2 0.6 gather_fusion
  16.8 11.1 %gather_fusion.1 = bf16[2048,256]{1,0:T(8,128)(2,1)S(1)} fusion(bf16[16384,256]{1,0:T(8,128)(2,1)} %param.19, s32[2048]{0:T(1024)S(1)} %fusion.3), kind=kCustom, calls=%fused_computation.1 | custom fusion | bytes 2105344 | tf_op jit(solution)/shard_map/jit(_take)/gather | solution.py:534
  27.9 0.0 copy-done
  27.9 0.0 copy-start.11
  27.9 0.0 copy-start.12
  27.9 0.0 copy-start.10
  27.9 0.0 copy-start.8
  27.9 0.0 copy-start.9
  27.9 1.5 %fusion.emb_ref = bf16[2048,256]{1,0:T(8,128)(2,1)} fusion(bf16[32,256]{1,0:T(8,128)(2,1)S(1)} %copy-done, bf16[2048,256]{1,0:T(8,128)(2,1)S(1)} %gather_fusion.1, s32[2048]{0:T(1024)S(1)} %get-tuple-element.14), kind=kOutput, calls=%fused_computation.3 | convolution fusion | flops 35192832 | bytes 2121728 | tf_op jit(solution)/shard_map/dot_general | solution.py:535
  29.5 0.0 copy-done.11
  29.5 0.1 copy.23
  29.6 0.0 copy-done.12
  29.7 0.0 copy-done.10
  29.7 0.8 pad_maximum_fusion.w_ref
  30.4 73.8 %gather_weights_and_embedded.1 = (bf16[4,5,1024,256]{3,2,1,0:T(8,128)(2,1)}, bf16[4,512,256]{2,1,0:T(8,128)(2,1)}) custom-call(bf16[5,128,256]{2,1,0:T(8,128)(2,1)} %pad_maximum_fusion.w_ref, bf16[2048,256]{1,0:T(8,128)(2,1)} %fusion.emb_ref), custom_call_target="tpu_custom_call" | custom-call | tf_op jit(solution)/shard_map/gather_weights_and_embedded/pallas_call | solution.py:539
  104.2 0.1 fusion.2.hit_ref
  104.4 0.0 copy-done.8
  104.4 0.0 copy-done.9
  104.4 0.0 copy-start.4
  104.4 1.2 copy-done.4
  105.6 12.2 %encode.1.kv_ref = bf16[4,512,256]{2,1,0:T(8,128)(2,1)S(1)} custom-call(f32[8]{0:T(128)S(1)} %copy-done.9, bf16[4,512,256]{2,1,0:T(8,128)(2,1)S(1)} %copy-done.4, f32[1,1024]{1,0:T(1,128)S(1)} %bitcast.26, bf16[4,5,1024,256]{3,2,1,0:T(8,128)(2,1)} %get-tuple-element.11.w_ref.cca_ref, bf16[4,5,1024,256]{3,2,1,0:T(8,128)(2,1)} %get-tuple-element.11.w_ref.cca_ref, ...), custom_call_target="tpu_custom_call" | custom-call | tf_op jit(solution)/shard_map/encode/pallas_call | solution.py:559
  117.9 0.0 copy-start.2
  117.9 1.0 copy-done.2
  118.9 0.0 copy-start.13
  118.9 0.0 copy-start.3
  118.9 16.9 %spread_keys_values.1.prev_ref.cur_ref = bf16[2304,256]{1,0:T(8,128)(2,1)} custom-call(bf16[4,512,256]{2,1,0:T(8,128)(2,1)} %copy-done.2), custom_call_target="tpu_custom_call" | custom-call | tf_op jit(solution)/shard_map/spread_keys_values/pallas_call | solution.py:586
  135.8 0.0 copy-done.13
  135.8 0.0 copy-done.3
  135.8 0.0 copy-start.1
  135.9 1.3 copy-done.1
  137.1 7.1 %attend.1 = bf16[512,1024]{1,0:T(8,128)(2,1)} custom-call(s32[8]{0:T(128)S(1)} %and_convert_fusion.allowed_ref, bf16[512,1024]{1,0:T(8,128)(2,1)S(1)} %copy-done.3, bf16[2304,256]{1,0:T(8,128)(2,1)S(1)} %copy-done.1, bf16[2304,256]{1,0:T(8,128)(2,1)S(1)} %copy-done.1), custom_call_target="tpu_custom_call" | custom-call | tf_op jit(solution)/shard_map/attend/pallas_call | solution.py:599
  (9 shorter events, 0.1 us)
Async XLA Ops:
  0.0 27.9 %copy-start = (bf16[32,256]{1,0:T(8,128)(2,1)S(1)}, bf16[32,256]{1,0:T(8,128)(2,1)}, u32[]{:S(2)}) copy-start(bf16[32,256]{1,0:T(8,128)(2,1)} %param.20) | copy-start | bytes 49156
  2.4 1.0 copy-start.5
  3.4 0.9 copy-start.6
  4.3 0.9 copy-start.7
  27.9 1.6 %copy-start.11 = (bf16[256,128]{1,0:T(8,128)(2,1)S(1)}, bf16[256,128]{1,0:T(8,128)(2,1)}, u32[]{:S(2)}) copy-start(bf16[256,128]{1,0:T(8,128)(2,1)} %param.24) | copy-start | bytes 196612
  27.9 1.7 %copy-start.12 = (bf16[128,2,128]{2,1,0:T(2,128)(2,1)S(1)}, bf16[128,2,128]{2,1,0:T(2,128)(2,1)}, u32[]{:S(2)}) copy-start(bf16[128,2,128]{2,1,0:T(2,128)(2,1)} %param.27) | copy-start | bytes 196612
  27.9 1.8 %copy-start.10 = (bf16[128,3,256]{2,0,1:T(8,128)(2,1)S(1)}, bf16[128,3,256]{2,0,1:T(8,128)(2,1)}, u32[]{:S(2)}) copy-start(bf16[128,3,256]{2,0,1:T(8,128)(2,1)} %param.22) | copy-start | bytes 589828
  27.9 76.5 %copy-start.8 = (f32[1024]{0:T(1024)S(1)}, f32[1024]{0:T(1024)}, u32[]{:S(2)}) copy-start(f32[1024]{0:T(1024)} %param.21) | copy-start | bytes 12292
  27.9 76.5 %copy-start.9 = (f32[8]{0:T(128)S(1)}, f32[8]{0:T(128)}, u32[]{:S(2)}) copy-start(f32[8]{0:T(128)} %bias_ref.1) | copy-start | bytes 100
  104.4 1.2 copy-start.4
  117.9 1.0 copy-start.2
  118.9 17.0 %copy-start.13 = (s32[8]{0:T(128)S(1)}, s32[8]{0:T(128)}, u32[]{:S(2)}) copy-start(s32[8]{0:T(128)} %param.18) | copy-start | bytes 100
  118.9 17.0 %copy-start.3 = (bf16[512,1024]{1,0:T(8,128)(2,1)S(1)}, bf16[512,1024]{1,0:T(8,128)(2,1)}, u32[]{:S(2)}) copy-start(bf16[512,1024]{1,0:T(8,128)(2,1)} %q_ref.1) | copy-start | bytes 3145732
  135.8 1.3 copy-start.1

commit v3 on v2

--- a/solution.py
+++ b/solution.py
@@ -23,9 +23,16 @@
 
 
 def fetch_kernel(
-    seq_size, tp_size, req_ref, tok_ref, dep_ref, par_ref, cond_ref, resp_ref, cond_out, asked, answer, own_sem, q_send, q_recv, r_send, r_recv, c_send, c_recv
+    seq_size, tp_size, req_ref, tok_hbm, dep_hbm, par_hbm, cond_ref, resp_ref, cond_out, asked, answer, tok_ref, dep_ref, par_ref, load_sem, own_sem, q_send, q_recv, r_send, r_recv, c_send, c_recv
 ):
     s, t = lax.axis_index("seq"), lax.axis_index("tp")
+    loads = []
+    for index, (source, held) in enumerate(
+        ((tok_hbm, tok_ref), (dep_hbm, dep_ref), (par_hbm, par_ref))
+    ):
+        copy = pltpu.make_async_copy(source, held, load_sem.at[index])
+        copy.start()
+        loads.append(copy)
     seq_peers = [(lax.rem(s + j, seq_size), t) for j in range(1, seq_size)]
     tp_peers = [(s, lax.rem(t + j, tp_size)) for j in range(1, tp_size)]
     enter(seq_peers + tp_peers)
@@ -61,7 +68,7 @@
     kept = copy
 
     asked[s] = req_ref[s]
-    for copy in requests:
+    for copy in requests + loads:
         copy.wait()
     places = asked[...].reshape(seq_size * 8, 128)[:, :1]
     stored = tok_ref.shape[0]
@@ -501,11 +508,15 @@
             jax.ShapeDtypeStruct((seq_size, 8, 384), jnp.int32),
             jax.ShapeDtypeStruct((tp_size, 2, block_share * cond_len, part), bf16),
         ),
-        in_specs=[vmem] * 4 + [anywhere],
+        in_specs=[vmem] + [anywhere] * 4,
         out_specs=(vmem, anywhere),
         scratch_shapes=[
             pltpu.VMEM((seq_size, 8, 128), jnp.int32),
             pltpu.VMEM((seq_size, 8, 384), jnp.int32),
+            pltpu.VMEM((stored, length), jnp.int32),
+            pltpu.VMEM((stored, length), jnp.int32),
+            pltpu.VMEM((stored, length), jnp.int32),
+            dma((3,)),
             dma,
             dma((seq_size,)),
             dma((seq_size,)),
@@ -578,7 +589,7 @@
             pltpu.VMEM((mine, part), bf16),
             pltpu.VMEM((mine, part), bf16),
         ],
-        compiler_params=pltpu.CompilerParams(vmem_limit_bytes=48 << 20),
+        compiler_params=pltpu.CompilerParams(vmem_limit_bytes=56 << 20),
         name="encode",
     )(tree_bias, own_emb, enc_gain.reshape(1, width), full, full, cond_blocks, hit)
 
@@ -589,7 +600,7 @@
         in_specs=[anywhere],
         out_specs=anywhere,
         scratch_shapes=[dma((tp_size,)), dma((tp_size,)), dma((tp_size,)), dma, dma],
-        compiler_params=pltpu.CompilerParams(collective_id=2, has_side_effects=True),
+        compiler_params=pltpu.CompilerParams(collective_id=2, has_side_effects=True, vmem_limit_bytes=56 << 20),
         name="spread_keys_values",
     )(keys_values)
 
@@ -607,7 +618,7 @@
             pl.BlockSpec((key_rows, part), lambda i: (i + 1, 0)),
         ],
         out_specs=pl.BlockSpec((cond_len, columns), lambda i: (i, 0)),
-        compiler_params=pltpu.CompilerParams(vmem_limit_bytes=32 << 20),
+        compiler_params=pltpu.CompilerParams(vmem_limit_bytes=56 << 20),
         name="attend",
     )(allowed, queries, spread, spread)
 

time: 145 us -> 146 us (level)
  Pallas kernels: 121 us -> 124 us
  local copies, waits for them, and re-layouts: 20.4 us -> 17.7 us
    unnamed x31 -> x21, local copies, waits for them, and re-layouts: 8.33 us -> 5.65 us
    pallas_call x1, Pallas kernels: 7.11 us -> 8.7 us  [shards(): pl.pallas_call(attend_kernel, grid=(block_count,), out_shape=jax.ShapeDty...]
where the time goes in v3:
time: 146 us
  Pallas kernels  124 us (85%)
  local copies, waits for them, and re-layouts  17.7 us (12%)
  other arithmetic  2.45 us (2%)
  matrix products  1.54 us (1%)
    pallas_call x1, Pallas kernels, shards(): pl.pallas_call(functools.partial(gather_kernel, seq_size, tp_size), out_s...  73.8 us
    pallas_call x1, Pallas kernels, shards(): pl.pallas_call(functools.partial(spread_kernel, seq_size, tp_size), out_s...  16.9 us
    pallas_call x1, Pallas kernels, shards(): pl.pallas_call(functools.partial(encoder_kernel, tp_size, length, pair_co...  13.6 us
    gather x1, local copies, waits for them, and re-layouts, shards(): jnp.take(table, tokens, axis=0, mode='clip').astype(jnp.float32)  11.1 us
    pallas_call x1, Pallas kernels, shards(): pl.pallas_call(functools.partial(fetch_kernel, seq_size, tp_size), out_sh...  10.9 us
    pallas_call x1, Pallas kernels, shards(): pl.pallas_call(attend_kernel, grid=(block_count,), out_shape=jax.ShapeDty...  8.7 us
    unnamed x21, local copies, waits for them, and re-layouts  5.65 us

profile of v3, /device:TPU:13, one launch (start us, length us, event | category | flops | bytes accessed | tf_op | source)
XLA Modules:
  0.0 145.8 jit_solution(11855703675666730610)
XLA Ops:
  0.0 0.0 copy-start
  0.0 0.8 copy.24
  0.8 0.1 reshape.175
  0.9 0.2 convert_reduce_fusion
  1.1 0.1 select_reduce_fusion
  1.1 0.1 broadcast_in_dim.41
  1.2 0.1 broadcast_in_dim.42.req_ref
  1.3 1.1 copy.28
  2.4 0.0 copy-start.2
  2.4 0.9 copy-done.2
  3.4 0.0 copy-start.3
  3.4 0.9 copy-done.3
  4.3 0.0 copy-start.4
  4.3 0.9 copy-done.4
  5.3 10.9 %fetch_rows.1 = (s32[8,8,384]{2,1,0:T(8,128)S(1)}, bf16[4,2,128,256]{3,2,1,0:T(8,128)(2,1)S(1)}) custom-call(s32[8,8,128]{2,1,0:T(8,128)S(1)} %broadcast_in_dim.42.req_ref, s32[512,128]{1,0:T(8,128)S(1)} %copy-done.2, s32[512,128]{1,0:T(8,128)S(1)} %copy-done.3, s32[512,128]{1,0:T(8,128)S(1)} %copy-done.4, bf16[2,512,256]{2,1,0:T(8,128)(2,1)S(1)} %bitcast.23), custom_call_target="tpu_custom_call" | custom-call | tf_op jit(solution)/shard_map/fetch_rows/pallas_call | solution.py:505
  16.2 0.0 copy-start.1
  16.2 0.8 copy-done.1
  16.9 0.1 reshape.177
  17.0 0.6 gather_fusion
  17.7 11.1 %gather_fusion.1 = bf16[2048,256]{1,0:T(8,128)(2,1)S(1)} fusion(bf16[16384,256]{1,0:T(8,128)(2,1)} %param.19, s32[2048]{0:T(1024)S(1)} %fusion.3), kind=kCustom, calls=%fused_computation.1 | custom fusion | bytes 2105344 | tf_op jit(solution)/shard_map/jit(_take)/gather | solution.py:545
  28.8 0.0 copy-done
  28.8 0.0 copy-start.6
  28.8 0.0 copy-start.7
  28.8 0.0 copy-start.5
  28.8 1.5 %fusion.emb_ref = bf16[2048,256]{1,0:T(8,128)(2,1)} fusion(bf16[32,256]{1,0:T(8,128)(2,1)S(1)} %copy-done, bf16[2048,256]{1,0:T(8,128)(2,1)S(1)} %gather_fusion.1, s32[2048]{0:T(1024)S(1)} %get-tuple-element.14), kind=kOutput, calls=%fused_computation.3 | convolution fusion | flops 35192832 | bytes 2121728 | tf_op jit(solution)/shard_map/dot_general | solution.py:546
  30.3 0.0 copy-done.6
  30.3 0.1 copy.23
  30.5 0.0 copy-done.7
  30.5 0.0 copy-done.5
  30.5 0.8 pad_maximum_fusion.w_ref
  31.3 73.8 %gather_weights_and_embedded.1 = (bf16[4,5,1024,256]{3,2,1,0:T(8,128)(2,1)}, bf16[4,512,256]{2,1,0:T(8,128)(2,1)}) custom-call(bf16[5,128,256]{2,1,0:T(8,128)(2,1)} %pad_maximum_fusion.w_ref, bf16[2048,256]{1,0:T(8,128)(2,1)} %fusion.emb_ref), custom_call_target="tpu_custom_call" | custom-call | tf_op jit(solution)/shard_map/gather_weights_and_embedded/pallas_call | solution.py:550
  105.1 0.8 fusion.2.hit_ref
  105.9 13.6 %encode.1.kv_ref = bf16[4,512,256]{2,1,0:T(8,128)(2,1)} custom-call(f32[8]{0:T(128)} %bias_ref.1, bf16[4,512,256]{2,1,0:T(8,128)(2,1)} %get-tuple-element.10.emb_ref, f32[1,1024]{1,0:T(1,128)} %bitcast.28, bf16[4,5,1024,256]{3,2,1,0:T(8,128)(2,1)} %get-tuple-element.11.w_ref.cca_ref, bf16[4,5,1024,256]{3,2,1,0:T(8,128)(2,1)} %get-tuple-element.11.w_ref.cca_ref, ...), custom_call_target="tpu_custom_call" | custom-call | tf_op jit(solution)/shard_map/encode/pallas_call | solution.py:570
  119.5 0.0 copy-start.8
  119.5 16.9 %spread_keys_values.1.prev_ref.cur_ref = bf16[2304,256]{1,0:T(8,128)(2,1)} custom-call(bf16[4,512,256]{2,1,0:T(8,128)(2,1)} %encode.1.kv_ref), custom_call_target="tpu_custom_call" | custom-call | tf_op jit(solution)/shard_map/spread_keys_values/pallas_call | solution.py:597
  136.5 0.0 copy-done.8
  136.5 0.5 and_convert_fusion.allowed_ref
  137.1 8.7 %attend.1 = bf16[512,1024]{1,0:T(8,128)(2,1)} custom-call(s32[8]{0:T(128)} %and_convert_fusion.allowed_ref, bf16[512,1024]{1,0:T(8,128)(2,1)} %q_ref.1, bf16[2304,256]{1,0:T(8,128)(2,1)} %spread_keys_values.1.prev_ref.cur_ref, bf16[2304,256]{1,0:T(8,128)(2,1)} %spread_keys_values.1.prev_ref.cur_ref), custom_call_target="tpu_custom_call" | custom-call | tf_op jit(solution)/shard_map/attend/pallas_call | solution.py:610
  (8 shorter events, 0.1 us)
Async XLA Ops:
  0.0 28.8 %copy-start = (bf16[32,256]{1,0:T(8,128)(2,1)S(1)}, bf16[32,256]{1,0:T(8,128)(2,1)}, u32[]{:S(2)}) copy-start(bf16[32,256]{1,0:T(8,128)(2,1)} %param.20) | copy-start | bytes 49156
  2.4 1.0 copy-start.2
  3.4 0.9 copy-start.3
  4.3 0.9 copy-start.4
  16.2 0.8 copy-start.1
  28.8 1.6 %copy-start.6 = (bf16[256,128]{1,0:T(8,128)(2,1)S(1)}, bf16[256,128]{1,0:T(8,128)(2,1)}, u32[]{:S(2)}) copy-start(bf16[256,128]{1,0:T(8,128)(2,1)} %param.24) | copy-start | bytes 196612
  28.8 1.7 %copy-start.7 = (bf16[128,2,128]{2,1,0:T(2,128)(2,1)S(1)}, bf16[128,2,128]{2,1,0:T(2,128)(2,1)}, u32[]{:S(2)}) copy-start(bf16[128,2,128]{2,1,0:T(2,128)(2,1)} %param.27) | copy-start | bytes 196612
  28.8 1.7 %copy-start.5 = (bf16[128,3,256]{2,0,1:T(8,128)(2,1)S(1)}, bf16[128,3,256]{2,0,1:T(8,128)(2,1)}, u32[]{:S(2)}) copy-start(bf16[128,3,256]{2,0,1:T(8,128)(2,1)} %param.22) | copy-start | bytes 589828
  119.5 16.9 %copy-start.8 = (s32[8]{0:T(128)S(1)}, s32[8]{0:T(128)}, u32[]{:S(2)}) copy-start(s32[8]{0:T(128)} %param.18) | copy-start | bytes 100
